TPU v7x, 256 devices: a whole 4x4x8 slice. The times are simulated.
256 devices in a mesh: row: 32 (over x_hi, z, core), rep: 8 (over x_lo, y).
Axes of the slice: x: 4 (x_hi: 2, x_lo: 2; x = x_hi * 2 + x_lo), y: 4, z: 8, core: 2. Of those that a mesh axis runs over, the one named last changes fastest.
Arguments:
- features: bfloat16 [32768, 128], P('row'), may hold values from -6 to 6
- adj_tiles: bfloat16 [32, 8, 4, 32, 128, 128], P('row', 'rep'), may hold values from -0.0625 to 0.0625
- tile_coords: int32 [32, 8, 4, 32, 2], P('row', 'rep'), may hold values from 0 to 7, as said below
- tile_counts: int32 [32, 8, 4], P('row', 'rep'), may hold values from 1 to 32, as said below
- weight: bfloat16 [128, 256], replicated, may hold values from -0.5 to 0.5
- out_bias: float32 [256], replicated, may hold values from -3 to 3
- out_grad: bfloat16 [32768, 256], P(('row', 'rep')), may hold values from -0.032958984 to 0.032958984
Outputs:
- activated: bfloat16 [32768, 256], P(('row', 'rep'))
- weight_grad: float32 [128, 256], replicated
- bias_grad: float32 [256], replicated
Inputs may be any that keep to these rules, and one draw needn't show every extreme that they name: `tile_coords`: within one block pair the live slots name distinct tiles; dead slots name valid tiles too. `tile_counts`: some block pair is full in every draw.
All inputs are finite; a program needn't handle non-finite values.
Results may differ from a plain program's by a relative error of at most 0.007.
Values may be sent and summed in bfloat16 or wider, within the bound.
A program may use at most 64 MiB of HBM per device.

v0:
```python
import jax
import jax.numpy as jnp
from jax import lax
from jax.sharding import PartitionSpec as P


def spread(value, axis, root):
    mine = lax.axis_index(axis) == root
    return lax.psum(jnp.where(mine, value, jnp.zeros_like(value)), axis)


def place_rows(tile_products, rows, live_mask, blocks):
    placement = ((rows[..., None] == jnp.arange(blocks)) & live_mask[..., None]).astype(jnp.float32)
    return jnp.einsum("scr,scaf->raf", placement, tile_products, precision=lax.Precision.HIGHEST)


def shards(features, adj_tiles, tile_coords, tile_counts, weight, out_bias, out_grad):
    resident_tiles = adj_tiles[0, 0]
    coords = tile_coords[0, 0]
    counts = tile_counts[0, 0]
    section_count = resident_tiles.shape[0]
    slot_count = resident_tiles.shape[1]
    tile_size = resident_tiles.shape[2]
    node_rows = features.shape[0]
    feat_width = features.shape[1]
    blocks = node_rows // tile_size
    rep_size = lax.axis_size("rep")
    rep_index = lax.axis_index("rep")
    live_mask = jnp.arange(slot_count)[None, :] < counts[:, None]
    own_blocks = features.reshape(blocks, tile_size, feat_width)
    partial_sum = jnp.zeros((blocks, tile_size, feat_width), jnp.float32)
    for graph_portion in range(section_count):
        root_index = graph_portion * rep_size + rep_index
        arrived = spread(own_blocks, "row", root_index)
        selected_entries = arrived[coords[graph_portion, :, 1]]
        tile_products = jnp.einsum(
            "wyh,whz->wyz",
            resident_tiles[graph_portion],
            selected_entries,
            preferred_element_type=jnp.float32,
        )
        partial_sum = partial_sum + place_rows(
            tile_products[None],
            coords[graph_portion : graph_portion + 1, :, 0],
            live_mask[graph_portion : graph_portion + 1],
            blocks,
        )
    partial_sum = partial_sum.reshape(node_rows, feat_width)
    share_rows = node_rows // rep_size
    reduced_total = lax.psum(partial_sum, "rep")
    common_node_rows = lax.dynamic_slice_in_dim(
        reduced_total, rep_index * share_rows, share_rows, 0
    )
    aggregated = common_node_rows.astype(jnp.bfloat16)
    pre_act = jnp.dot(aggregated, weight, preferred_element_type=jnp.float32) + out_bias
    activated = jax.nn.silu(pre_act).astype(jnp.bfloat16)
    sigmoid_pre = jax.nn.sigmoid(pre_act)
    grad_pre = (
        out_grad.astype(jnp.float32) * sigmoid_pre * (1.0 + pre_act * (1.0 - sigmoid_pre))
    ).astype(jnp.bfloat16)
    weight_part = lax.dot_general(
        aggregated, grad_pre, (((0,), (0,)), ((), ())), preferred_element_type=jnp.float32
    )
    bias_part = jnp.sum(grad_pre.astype(jnp.float32), axis=0)
    weight_grad, bias_grad = lax.psum((weight_part, bias_part), ("row", "rep"))
    return (activated, weight_grad, bias_grad)


def solution(mesh):
    placed = (
        P("row", None),
        P("row", "rep", None, None, None, None),
        P("row", "rep", None, None, None),
        P("row", "rep", None),
        P(),
        P(),
        P(("row", "rep"), None),
    )
    return jax.shard_map(
        shards,
        mesh=mesh,
        in_specs=placed,
        out_specs=(P(("row", "rep"), None), P(), P()),
        check_vma=False,
    )
```

profile of v0, /device:TPU:1, one launch (start us, length us, event | category | flops | bytes accessed | tf_op | source)
XLA Modules:
  0.0 602.6 jit_solution(11005349123491617999)
XLA Ops:
  7.2 0.0 all-reduce.7.cloned.1.call-start
  7.3 2.0 broadcast_select_fusion
  9.2 0.0 all-reduce.7.cloned.1.call-update
  9.2 0.0 all-reduce.5.cloned.1.call-start
  9.4 0.1 iota_compare_fusion.4
  9.5 274.1 %all-reduce.7.cloned.1.call-done = (bf16[8,128,128]{2,1,0:T(8,128)(2,1)}, bf16[8,128,128]{2,1,0:T(8,128)(2,1)}, bf16[8,128,128]{2,1,0:T(8,128)(2,1)}, bf16[8,128,128]{2,1,0:T(8,128)(2,1)}) async-done(((bf16[8,128,128]{2,1,0:T(8,128)(2,1)}, bf16[8,128,128]{2,1,0:T(8,128)(2,1)}, bf16[8,128,128]{2,1,0:T(8,128)(2,1)}, bf16[8,128,128]{2,1,0:T(8,128)(2,1)}), (bf16[8,128,128]{2,1,0:T(8,128)(2,1)}, ...) | async-done | bytes 1048592 | tf_op jit(solution)/shard_map/psum | solution.py:9
  283.5 1.7 gather_fusion.1
  285.2 3.4 fusion.21
  288.7 2.4 copy.12
  291.1 0.7 gather_fusion
  291.9 3.4 fusion.23
  295.3 3.2 copy.11
  298.4 0.7 gather_fusion.2
  299.2 3.4 fusion.19
  302.6 3.1 copy.13
  305.7 0.7 gather_fusion.3
  306.5 3.5 fusion.17
  310.0 3.1 copy.14
  313.1 0.8 fusion.4
  313.9 0.7 copy-done.1
  314.7 0.8 fusion.8
  315.5 0.1 copy-done.2
  315.7 0.8 fusion.11
  316.5 0.6 copy-done.3
  317.2 0.8 fusion.14
  318.0 0.1 copy.10
  318.1 32.1 %all-reduce.8 = bf16[1024,128]{1,0:T(8,128)(2,1)S(1)} all-reduce(f32[1024,128]{1,0:T(8,128)S(1)} %bitcast.95), channel_id=1, replica_groups=mesh['row'=32,'rep'=8] {'rep'}, use_global_device_ids=true, to_apply=%region_4.5 | all-reduce | flops 131072 | bytes 786432 | tf_op jit(solution)/shard_map/psum | solution.py:50
  350.2 0.8 convert_reduce_fusion
  351.0 0.9 fusion.29
  351.9 81.0 %psum.55 = f32[256]{0:T(256)} all-reduce(f32[256]{0:T(256)S(1)} %get-tuple-element.7), channel_id=1, replica_groups=mesh['row'=32,'rep'=8] {'row','rep'}, use_global_device_ids=true, to_apply=%region_7.8 | all-reduce | flops 256 | bytes 2048 | tf_op jit(solution)/shard_map/psum | solution.py:65
  432.9 161.3 %all-reduce.5.cloned.1.call-done = f32[128,256]{1,0:T(8,128)} async-done(((f32[128,256]{1,0:T(8,128)}), f32[128,256]{1,0:T(8,128)}) %all-reduce.5.cloned.1.call-update) | async-done | bytes 131088 | tf_op jit(solution)/shard_map/psum | solution.py:65
  594.2 1.6 copy.22
  (25 shorter events, 0.1 us)
Async XLA Ops:
  7.2 343.0 %copy-start = (bf16[128,256]{1,0:T(8,128)(2,1)S(1)}, bf16[128,256]{1,0:T(8,128)(2,1)}, u32[]{:S(2)}) copy-start(bf16[128,256]{1,0:T(8,128)(2,1)} %param.11) | copy-start | bytes 196612
  7.2 2.1 copy-start.7
  7.2 2.2 copy-start.10
  7.2 276.3 %all-reduce.7.cloned.1.call-start = ((), (), s32[]{:S(2)}) async-start(), calls=%async_computation.1 | async-start | bytes 2097152 | tf_op jit(solution)/shard_map/psum | solution.py:9
  9.2 585.0 %all-reduce.5.cloned.1.call-start = ((), (), s32[]{:S(2)}) async-start(), calls=%async_computation | async-start | bytes 262144 | tf_op jit(solution)/shard_map/psum | solution.py:65
  288.7 2.4 copy-start.6
  295.3 3.2 copy-start.5
  302.6 3.1 copy-start.4
  313.1 1.6 copy-start.1
  313.9 1.7 copy-start.2
  315.5 1.6 copy-start.3
  317.1 33.0 %copy-start.8 = (bf16[128,256]{1,0:T(8,128)(2,1)S(1)}, bf16[128,256]{1,0:T(8,128)(2,1)}, u32[]{:S(2)}) copy-start(bf16[128,256]{1,0:T(8,128)(2,1)} %param.13) | copy-start | bytes 196612
  317.2 33.0 %copy-start.9 = (f32[256]{0:T(256)S(1)}, f32[256]{0:T(256)}, u32[]{:S(2)}) copy-start(f32[256]{0:T(256)} %param.12) | copy-start | bytes 3076
Sparse Core Ops, SparseCore 0:
  10.9 272.5 all-reduce.6
  352.0 242.1 all-reduce.4
where the time goes:
time: 603 us
  waiting for transfers between devices  435 us (72%)
  blocking collectives  113 us (19%)
  local copies, waits for them, and re-layouts  19 us (3%)
  matrix products  18.8 us (3%)
  between operations  14.2 us (2%)
    psum x1, waiting for transfers between devices, spread(): return lax.psum(jnp.where(mine, value, jnp.zeros_like(value)), axis)  274 us
    psum x1, waiting for transfers between devices, shards(): weight_grad, bias_grad = lax.psum((weight_part, bias_part), ('row', 'rep'))  161 us
    psum x1, blocking collectives, shards(): weight_grad, bias_grad = lax.psum((weight_part, bias_part), ('row', 'rep'))  81 us
    psum x1, blocking collectives, shards(): reduced_total = lax.psum(partial_sum, 'rep')  32.1 us
    dot_general x4, matrix products, shards(): jnp.einsum('wyh,whz->wyz', resident_tiles[graph_portion], selected_entrie...  13.8 us
  transfers between devices with their start and end apart: 2, of which 2 were waited for; matrix products, arithmetic and copies ran while one was open for 0% of the time, Pallas kernels for 0%

commit v1 on v0

v1 whole, which is shorter than its diff:
```python
import functools

import jax
import jax.numpy as jnp
from jax import lax
from jax.experimental import pallas as pl
from jax.experimental.pallas import tpu as pltpu
from jax.sharding import PartitionSpec as P

MESH = pl.DeviceIdType.MESH
F32 = jnp.float32
BF16 = jnp.bfloat16

PLANE = sorted(
    [(dx, dy) for dx in range(4) for dy in range(4) if (dx, dy) != (0, 0)],
    key=lambda o: -(min(o[0], 4 - o[0]) + min(o[1], 4 - o[1])),
)
ALONG_Z = [4, 3, 5, 2, 6, 1, 7]
COLUMN = [(d, k) for d in ALONG_Z for k in (0, 1)] + [(0, 1)]


def layer_kernel(
    inv_ref,
    feat_ref,
    adj_ref,
    weight_ref,
    bias_ref,
    cot_ref,
    act_ref,
    wg_ref,
    bg_ref,
    tiles,
    held,
    feats,
    acc,
    part_out,
    part_in,
    c1_out,
    c1_in,
    c2_in,
    c3_in,
    tile_sem,
    a1_send,
    a1_recv,
    a2_send,
    a2_recv,
    a3_send,
    b_send,
    b_recv,
    c_send,
    c_recv,
):
    row = lax.axis_index("row")
    rep = lax.axis_index("rep")
    xh, z, core = row // 16, (row // 2) % 8, row % 2
    x, y = xh * 2 + rep // 4, rep % 4
    plane = x * 4 + y
    column = z * 2 + core

    def device(dx, dy, dz, dcore):
        x2, y2, z2, c2 = (x + dx) % 4, (y + dy) % 4, (z + dz) % 8, (core + dcore) % 2
        return (x2 // 2) * 16 + z2 * 2 + c2, (x2 % 2) * 4 + y2

    def remote(src, dst, send, recv, target):
        return pltpu.make_async_remote_copy(
            src_ref=src,
            dst_ref=dst,
            send_sem=send,
            recv_sem=recv,
            device_id=target,
            device_id_type=MESH,
        )

    def wait_bytes(ref, sem):
        pltpu.make_async_copy(ref, ref, sem).wait()

    live = tiles.shape[0] - 1
    tile_copy = pltpu.make_async_copy(adj_ref, tiles.at[pl.ds(0, live)], tile_sem)
    tile_copy.start()

    barrier = pltpu.get_barrier_semaphore()
    for dx, dy in PLANE:
        pl.semaphore_signal(barrier, inc=1, device_id=device(dx, dy, 0, 0), device_id_type=MESH)
    for dz, dcore in COLUMN:
        pl.semaphore_signal(barrier, inc=1, device_id=device(0, 0, dz, dcore), device_id_type=MESH)
    tiles[live] = jnp.zeros(tiles.shape[1:], BF16)
    c1_out[...] = jnp.zeros_like(c1_out)
    held[z % 4, z // 4] = feat_ref[rep]
    pl.semaphore_wait(barrier, len(PLANE) + len(COLUMN))

    sends = []
    for dz in ALONG_Z:
        copy = remote(
            feat_ref.at[rep], held.at[z % 4, z // 4], a1_send, a1_recv.at[z], device(0, 0, dz, 0)
        )
        copy.start()
        sends.append(copy)

    def to_users(step, target_xh):
        m = (z + step) % 4
        user = m * 2 + core
        mine = jnp.logical_and(user == rep, xh == target_xh)
        copy = remote(
            held.at[m],
            feats.at[pl.ds(xh * 2, 2), rep],
            a2_send,
            a2_recv.at[xh, rep],
            (target_xh * 16 + z * 2 + core, user),
        )
        local = pltpu.make_async_copy(
            held.at[m], feats.at[pl.ds(xh * 2, 2), rep], a2_recv.at[xh, rep]
        )
        return mine, copy, local

    for step in (0, 2, 1, 3):
        for half in (0, 4):
            dz = (step + half) % 8
            if dz:
                src = (z + dz) % 8
                wait_bytes(held.at[src % 4, src // 4], a1_recv.at[src])
        for target_xh in (0, 1):
            mine, copy, local = to_users(step, target_xh)

            @pl.when(jnp.logical_not(mine))
            def _():
                copy.start()

            @pl.when(mine)
            def _():
                local.start()

    primary = core == y % 2

    def pass_on(src_xh, q):
        piece = feats.at[pl.ds(src_xh * 2, 2), q]
        return remote(piece, piece, a3_send, a2_recv.at[src_xh, q], device(0, 0, 0, 1))

    tile_copy.wait()
    for src_xh in (0, 1):
        for q in range(8):
            wait_bytes(feats.at[pl.ds(src_xh * 2, 2), q], a2_recv.at[src_xh, q])

            @pl.when(primary)
            def _():
                pass_on(src_xh, q).start()

    def products(r, sections):
        total = None
        for t in sections:
            left = jnp.concatenate([tiles[inv_ref[t * 64 + r * 8 + q]] for q in range(8)], axis=1)
            right = feats[t].reshape(8 * 128, 128)
            term = jnp.dot(left, right, preferred_element_type=F32)
            total = term if total is None else total + term
        return total

    def send_part(r):
        return remote(part_out.at[r], part_in.at[rep], b_send, b_recv, (row, r))

    def tile_row(i, carry):
        r = (rep + 1 + i) % 8
        total = products(r, range(4))
        acc[r] = total
        part_out[r] = total.astype(BF16)

        @pl.when(r != rep)
        def _():
            send_part(r).start()

        return carry

    lax.fori_loop(0, 8, tile_row, 0)
    part_in[rep] = jnp.zeros(part_in.shape[1:], BF16)
    wait_bytes(part_in.at[pl.ds(0, 7)], b_recv)
    total = acc[rep]
    for s in range(8):
        total = total + part_in[s].astype(F32)

    aggregated = total.astype(BF16)
    pre = jnp.dot(aggregated, weight_ref[...], preferred_element_type=F32) + bias_ref[...]
    sig = jax.nn.sigmoid(pre)
    act_ref[...] = (pre * sig).astype(BF16)
    grad = (cot_ref[...].astype(F32) * sig * (1.0 + pre * (1.0 - sig))).astype(BF16)
    weight_part = lax.dot_general(
        aggregated, grad, (((0,), (0,)), ((), ())), preferred_element_type=F32
    )
    bias_part = jnp.sum(grad.astype(F32), axis=0, keepdims=True)

    c1_out[:, :, 0:256] = weight_part.reshape(16, 8, 256)
    for p in range(16):
        c1_out[p, 0:1, 256:384] = bias_part[:, 0:128]
        c1_out[p, 1:2, 256:384] = bias_part[:, 128:256]
    for dx, dy in PLANE:
        p = ((x + dx) % 4) * 4 + (y + dy) % 4
        remote(
            c1_out.at[p], c1_in.at[plane], c_send.at[0], c_recv.at[0], device(dx, dy, 0, 0)
        ).start()
    c1_in[plane] = c1_out[plane]
    wait_bytes(c1_in.at[pl.ds(0, 15)], c_recv.at[0])
    c2_in[column] = jnp.sum(c1_in[...], axis=0)
    for dz, dcore in COLUMN:
        remote(
            c2_in.at[column], c2_in.at[column], c_send.at[1], c_recv.at[1], device(0, 0, dz, dcore)
        ).start()
    wait_bytes(c2_in.at[pl.ds(0, 15)], c_recv.at[1])
    summed = jnp.sum(c2_in[...], axis=0)
    c3_in[plane] = summed[:, 0:256]
    for dx, dy in PLANE:
        remote(
            c3_in.at[plane], c3_in.at[plane], c_send.at[2], c_recv.at[2], device(dx, dy, 0, 0)
        ).start()
    bg_ref[:, 0:128] = summed[0:1, 256:384]
    bg_ref[:, 128:256] = summed[1:2, 256:384]
    wait_bytes(c3_in.at[pl.ds(0, 15)], c_recv.at[2])
    wg_ref[...] = c3_in[...].reshape(128, 256)

    for copy in sends:
        copy.wait_send()
    for step in (0, 2, 1, 3):
        for target_xh in (0, 1):
            mine, copy, local = to_users(step, target_xh)

            @pl.when(jnp.logical_not(mine))
            def _():
                copy.wait_send()

    @pl.when(primary)
    def _():
        for src_xh in (0, 1):
            for q in range(8):
                pass_on(src_xh, q).wait_send()

    wait_bytes(part_out.at[pl.ds(0, 7)], b_send)
    wait_bytes(c1_out.at[pl.ds(0, 15)], c_send.at[0])
    wait_bytes(c2_in.at[pl.ds(0, 15)], c_send.at[1])
    wait_bytes(c3_in.at[pl.ds(0, 15)], c_send.at[2])


def slot_of_tile(coords, counts):
    sections, slots = coords.shape[0], coords.shape[1]
    key = coords[:, :, 0] * 8 + coords[:, :, 1]
    live = jnp.arange(slots)[None, :] < counts[:, None]
    slot = jnp.arange(sections)[:, None] * slots + jnp.arange(slots)[None, :] - sections * slots
    hit = (key[:, None, :] == jnp.arange(64)[None, :, None]) & live[:, None, :]
    found = jnp.sum(jnp.where(hit, slot[:, None, :], 0), axis=-1) + sections * slots
    return found.reshape(sections * 64).astype(jnp.int32)


def shards(features, adj_tiles, tile_coords, tile_counts, weight, out_bias, out_grad):
    inv = slot_of_tile(tile_coords[0, 0], tile_counts[0, 0])
    vmem = pl.BlockSpec(memory_space=pltpu.VMEM)
    dma = pltpu.SemaphoreType.DMA
    activated, weight_grad, bias_grad = pl.pallas_call(
        layer_kernel,
        name="layer",
        out_shape=(
            jax.ShapeDtypeStruct((128, 256), BF16),
            jax.ShapeDtypeStruct((128, 256), F32),
            jax.ShapeDtypeStruct((1, 256), F32),
        ),
        in_specs=[
            pl.BlockSpec(memory_space=pltpu.SMEM),
            vmem,
            pl.BlockSpec(memory_space=pl.ANY),
            vmem,
            vmem,
            vmem,
        ],
        out_specs=(vmem, vmem, vmem),
        scratch_shapes=[
            pltpu.VMEM((129, 128, 128), BF16),
            pltpu.VMEM((4, 2, 128, 128), BF16),
            pltpu.VMEM((4, 8, 128, 128), BF16),
            pltpu.VMEM((8, 128, 128), F32),
            pltpu.VMEM((8, 128, 128), BF16),
            pltpu.VMEM((8, 128, 128), BF16),
            pltpu.VMEM((16, 8, 384), F32),
            pltpu.VMEM((16, 8, 384), F32),
            pltpu.VMEM((16, 8, 384), F32),
            pltpu.VMEM((16, 8, 256), F32),
            dma,
            dma,
            dma((8,)),
            dma,
            dma((2, 8)),
            dma,
            dma,
            dma,
            dma((3,)),
            dma((3,)),
        ],
        compiler_params=pltpu.CompilerParams(
            collective_id=1, has_side_effects=True, vmem_limit_bytes=56 << 20
        ),
        cost_estimate=pl.CostEstimate(
            flops=2 * 256 * 128**3, bytes_accessed=5 << 20, transcendentals=128 * 256
        ),
    )(
        inv,
        features.reshape(8, 128, 128),
        adj_tiles.reshape(128, 128, 128),
        weight,
        out_bias.reshape(1, 256),
        out_grad,
    )
    return activated, weight_grad, bias_grad.reshape(256)


def solution(mesh):
    placed = (
        P("row", None),
        P("row", "rep", None, None, None, None),
        P("row", "rep", None, None, None),
        P("row", "rep", None),
        P(),
        P(),
        P(("row", "rep"), None),
    )
    return jax.shard_map(
        shards,
        mesh=mesh,
        in_specs=placed,
        out_specs=(P(("row", "rep"), None), P(), P()),
        check_vma=False,
    )
```

time: 603 us -> 61.4 us (0.10)
  waiting for transfers between devices: 435 us -> 0 us
  blocking collectives: 113 us -> 0 us
  Pallas kernels: 0 us -> 53.9 us
  matrix products: 18.8 us -> 0 us
  local copies, waits for them, and re-layouts: 19 us -> 4.91 us
  between operations: 14.2 us -> 0.65 us
    psum x2 -> x0, waiting for transfers between devices: 435 us -> none  [the longest x1 274 us: spread(): return lax.psum(jnp.where(mine, value, jnp.zeros_like(value)), axis)]
    psum x2 -> x0, blocking collectives: 113 us -> none  [the longest x1 81 us: shards(): weight_grad, bias_grad = lax.psum((weight_part, bias_part), ('row', 'rep'))]
    pallas_call x0 -> x1, Pallas kernels: none -> 53.9 us  [shards(): pl.pallas_call(layer_kernel, name='layer', out_shape=(jax.ShapeDtypeStruc...]
    dot_general x10 -> x0, matrix products: 18.8 us -> none  [the longest x4 13.8 us: shards(): jnp.einsum('wyh,whz->wyz', resident_tiles[graph_portion], selected_entrie...]
    dot_general x4 -> x0, local copies, waits for them, and re-layouts: 11.8 us -> none  [shards(): jnp.einsum('wyh,whz->wyz', resident_tiles[graph_portion], selected_entrie...]
  transfers between devices with their start and end apart: 2 -> 0, of which waited for: 2 -> 0; matrix products, arithmetic and copies ran while one was open for 0% -> 0% of each run, Pallas kernels for 0% -> 0%
where the time goes in v1:
time: 61.4 us; the launch traced here: 61.2 us
  Pallas kernels  53.9 us (88%)
  local copies, waits for them, and re-layouts  4.91 us (8%)
  other arithmetic  1.71 us (3%)
  between operations  0.65 us (1%)
    pallas_call x1, Pallas kernels, shards(): pl.pallas_call(layer_kernel, name='layer', out_shape=(jax.ShapeDtypeStruc...  53.9 us
    unnamed x3, local copies, waits for them, and re-layouts  4.27 us

profile of v1, /device:TPU:1, one launch (start us, length us, event | category | flops | bytes accessed | tf_op | source)
XLA Modules:
  0.0 61.2 jit_solution(12746511838388327305)
XLA Ops:
  0.6 0.7 %iota_compare_fusion.1 = pred[4,32]{1,0:T(4,128)(4,1)S(1)} fusion(s32[4]{0:T(128)} %bitcast.13), kind=kLoop, calls=%fused_computation.6 | loop fusion | flops 128 | bytes 144 | tf_op jit(solution)/shard_map/lt | solution.py:241
  1.4 0.1 add_add_fusion
  1.4 0.8 %slice_add_fusion = s32[4,32,1]{1,2,0:T(1,128)S(1)} fusion(s32[4,32,2]{1,2,0:T(2,128)} %bitcast.10), kind=kLoop, calls=%fused_computation.3 | loop fusion | flops 256 | bytes 1536 | tf_op jit(solution)/shard_map/add | solution.py:240
  2.2 0.1 select_reduce_fusion
  2.3 0.6 %add.46.inv_ref = s32[256]{0:T(256)} reshape(s32[4,64]{1,0:T(4,128)S(1)} %broadcast_add_fusion) | data formatting | bytes 2048 | tf_op jit(solution)/shard_map/add | solution.py:244
  3.0 53.9 %layer.1 = (bf16[128,256]{1,0:T(8,128)(2,1)}, f32[128,256]{1,0:T(8,128)}, f32[1,256]{1,0:T(1,128)}) custom-call(s32[256]{0:T(256)} %add.46.inv_ref, bf16[8,128,128]{2,1,0:T(8,128)(2,1)} %bitcast.8, bf16[128,128,128]{2,1,0:T(8,128)(2,1)} %bitcast.7, bf16[128,256]{1,0:T(8,128)(2,1)} %weight_ref.1, f32[1,256]{1,0:T(1,128)} %bitcast.12, bf16[128,256]{1,0:T(8,128)(2,1)} %cot_ref.1), custom_call_target="tpu_custom_call" | custom-call | flops 1073741824 | bytes 5242880 | tf_op jit(solution)/shard_map/layer/pallas_call | solution.py:252
  56.9 1.5 %copy.13 = bf16[128,256]{1,0:T(8,128)(2,1)} copy(bf16[128,256]{1,0:T(8,128)(2,1)} %get-tuple-element.12) | data formatting | bytes 131072
  58.4 1.6 %copy.14 = f32[128,256]{1,0:T(8,128)} copy(f32[128,256]{1,0:T(8,128)} %get-tuple-element.13) | data formatting | bytes 262144
  60.0 1.2 %copy.15 = f32[256]{0:T(256)} copy(f32[256]{0:T(256)} %bitcast.11) | data formatting | bytes 2048
  (2 shorter events, 0.0 us)

commit v2 on v1

v2 whole, which is shorter than its diff:
```python
import functools

import jax
import jax.numpy as jnp
from jax import lax
from jax.experimental import pallas as pl
from jax.experimental.pallas import tpu as pltpu
from jax.sharding import PartitionSpec as P

MESH = pl.DeviceIdType.MESH
F32 = jnp.float32
BF16 = jnp.bfloat16

PLANE = sorted(
    [(dx, dy) for dx in range(4) for dy in range(4) if (dx, dy) != (0, 0)],
    key=lambda o: -(min(o[0], 4 - o[0]) + min(o[1], 4 - o[1])),
)
COLUMN = [(d, k) for d in (4, 3, 5, 2, 6, 1, 7) for k in (0, 1)] + [(0, 1)]


def layer_kernel(
    counts_ref,
    coords_ref,
    feat_ref,
    adj_ref,
    weight_ref,
    bias_ref,
    cot_ref,
    act_ref,
    wg_ref,
    bg_ref,
    tiles,
    slot_rows,
    slots,
    held,
    feats,
    acc,
    part_out,
    part_in,
    c1_out,
    c1_in,
    b1_out,
    b1_in,
    c2_in,
    c3_in,
    tile_sem,
    slot_sem,
    a1_send,
    a1_recv,
    a2_send,
    a2_recv,
    a3_send,
    b_send,
    b_recv,
    c_send,
    c_recv,
):
    row = lax.axis_index("row")
    rep = lax.axis_index("rep")
    xh, z, core = row // 16, (row // 2) % 8, row % 2
    xl, y = rep // 4, rep % 4
    x = xh * 2 + xl
    plane = x * 4 + y
    column = z * 2 + core
    live = tiles.shape[0] - 1

    def device(dx, dy, dz, dcore):
        x2, y2, z2, c2 = (x + dx) % 4, (y + dy) % 4, (z + dz) % 8, (core + dcore) % 2
        return (x2 // 2) * 16 + z2 * 2 + c2, (x2 % 2) * 4 + y2

    def remote(src, dst, send, recv, target):
        return pltpu.make_async_remote_copy(
            src_ref=src,
            dst_ref=dst,
            send_sem=send,
            recv_sem=recv,
            device_id=target,
            device_id_type=MESH,
        )

    def wait_bytes(ref, sem):
        pltpu.make_async_copy(ref, ref, sem).wait()

    pending = []
    tile_copy = pltpu.make_async_copy(adj_ref, tiles.at[pl.ds(0, live)], tile_sem)
    tile_copy.start()

    barrier = pltpu.get_barrier_semaphore()
    for dz, dcore in COLUMN:
        pl.semaphore_signal(barrier, inc=1, device_id=device(0, 0, dz, dcore), device_id_type=MESH)
    for dx, dy in PLANE:
        pl.semaphore_signal(barrier, inc=1, device_id=device(dx, dy, 0, 0), device_id_type=MESH)

    tiles[live] = jnp.zeros(tiles.shape[1:], BF16)
    lane = lax.broadcasted_iota(jnp.int32, (64, 32), 1)
    sub = lax.broadcasted_iota(jnp.int32, (64, 32), 0)
    wide_lane = lax.broadcasted_iota(jnp.int32, (64, 128), 1)
    wide_sub = lax.broadcasted_iota(jnp.int32, (64, 128), 0)
    for t in range(4):
        key = coords_ref[t, 0:1, :] * 8 + coords_ref[t, 1:2, :]
        hit = jnp.logical_and(key == sub, lane < counts_ref[t])
        found = jnp.sum(jnp.where(hit, lane + (t * 32 + 1), 0), axis=1, keepdims=True)
        turned = jnp.sum(jnp.where(wide_lane == wide_sub, found, 0), axis=0, keepdims=True)
        slot_rows[t : t + 1, :] = jnp.where(turned == 0, live, turned - 1)
    slot_copy = pltpu.make_async_copy(slot_rows, slots, slot_sem)
    slot_copy.start()

    flip = (core + xh) % 2

    @pl.when(xh == 0)
    def _():
        held[z] = feat_ref[rep]

    b1_out[...] = jnp.zeros_like(b1_out)
    part_in[rep] = jnp.zeros(part_in.shape[1:], BF16)
    pl.semaphore_wait(barrier, len(PLANE) + len(COLUMN))

    def along_z(dz):
        place = held.at[z]
        return remote(feat_ref.at[rep], place, a1_send.at[dz], a1_recv.at[z], device(0, 0, dz, xh))

    def pass_along(dz, to, first, rows):
        src = (z + dz) % 8
        piece = held.at[src, pl.ds(first, rows)]
        return remote(piece, piece, a1_send.at[8 + to % 8], a1_recv.at[src], device(0, 0, to, 0))

    def launch(copy):
        copy.start()
        pending.append(copy.wait_send)

    @pl.when(xh == 1)
    def _():
        along_z(0).start()

    pending.append(lambda: pl.when(xh == 1)(lambda: along_z(0).wait_send()))
    for dz in (2, 6, 1, 7):
        launch(along_z(dz))

    def to_user(dz, target_xh, start):
        src = (z + dz) % 8
        user = (src % 4) * 2 + flip
        mine = jnp.logical_and(user == rep, xh == target_xh)
        piece = held.at[src]
        section = xh * 2 + src // 4
        place = feats.at[section, rep]

        @pl.when(jnp.logical_not(mine))
        def _():
            copy = remote(
                piece,
                place,
                a2_send.at[dz, target_xh],
                a2_recv.at[section],
                (target_xh * 16 + z * 2 + core, user),
            )
            if start:
                copy.start()
            else:
                copy.wait_send()

        if start:

            @pl.when(mine)
            def _():
                pltpu.make_async_copy(piece, place, a2_recv.at[section]).start()

    def to_users(dz):
        for target_xh in (0, 1):
            to_user(dz, target_xh, True)
            pending.append(functools.partial(to_user, dz, target_xh, False))

    def wait_piece(dz):
        src = (z + dz) % 8
        wait_bytes(held.at[src], a1_recv.at[src])

    pl.when(xh == 1)(lambda: wait_piece(0))
    to_users(0)
    wait_piece(2)
    launch(pass_along(2, -2, 0, 64))
    launch(pass_along(2, -1, 0, 128))
    wait_piece(6)
    launch(pass_along(6, 2, 64, 64))
    launch(pass_along(6, 1, 0, 128))
    for dz in (1, 7):
        wait_piece(dz)
        to_users(dz)
    for dz in (2, 6):
        to_users(dz)
    for dz in (3, 5, 4):
        wait_piece(dz)
        to_users(dz)

    mine_xh = (core + y) % 2
    nearer = ((rep // 2 - z + 10) % 8) // 5
    own = [mine_xh * 2 + nearer, mine_xh * 2 + 1 - nearer]
    other = [2 - mine_xh * 2 + nearer, 3 - mine_xh * 2 - nearer]

    def arrive(section):
        wait_bytes(feats.at[section], a2_recv.at[section])

    def pass_on(section):
        piece = feats.at[section]
        launch(remote(piece, piece, a3_send.at[section], a2_recv.at[section], device(0, 0, 0, 1)))

    def products(r, section):
        left = jnp.concatenate([tiles[slots[section, r * 8 + q]] for q in range(8)], axis=1)
        right = feats[section].reshape(8 * 128, 128)
        return jnp.dot(left, right, preferred_element_type=F32)

    def add_products(section, first):
        for r in range(8):
            term = products(r, section)
            acc[r] = term if first else acc[r] + term

    tile_copy.wait()
    slot_copy.wait()
    arrive(own[0])
    pass_on(own[0])
    add_products(own[0], True)
    arrive(own[1])
    pass_on(own[1])
    arrive(other[0])
    add_products(other[0], False)
    add_products(own[1], False)
    arrive(other[1])

    for i, k in enumerate((2, 1, 3, 0, 2, 1, 3, 0)):
        r = ((xl + 1 - i // 4) % 2) * 4 + (y + k) % 4
        total = acc[r] + products(r, other[1])
        if i < 7:
            part_out[r] = total.astype(BF16)
            remote(part_out.at[r], part_in.at[rep], b_send, b_recv, (row, r)).start()

    for finish in pending:
        finish()
    pending.clear()
    pending.append(lambda: wait_bytes(part_out.at[pl.ds(0, 7)], b_send))
    wait_bytes(part_in.at[pl.ds(0, 7)], b_recv)
    for s in range(8):
        total = total + part_in[s].astype(F32)

    aggregated = total.astype(BF16)
    pre = jnp.dot(aggregated, weight_ref[...], preferred_element_type=F32) + bias_ref[...]
    sig = jax.nn.sigmoid(pre)
    grad = (cot_ref[...].astype(F32) * sig * (1.0 + pre * (1.0 - sig))).astype(BF16)
    weight_part = lax.dot_general(
        aggregated, grad, (((0,), (0,)), ((), ())), preferred_element_type=F32
    )
    bias_part = jnp.sum(grad.astype(F32), axis=0, keepdims=True)

    owner = plane == 0
    c1_out[0:8] = weight_part[:, 0:128].astype(BF16).reshape(8, 16, 128)
    c1_out[8:16] = weight_part[:, 128:256].astype(BF16).reshape(8, 16, 128)
    b1_out[0:1, :] = bias_part[:, 0:128]
    b1_out[1:2, :] = bias_part[:, 128:256]

    def send_bias():
        return remote(
            b1_out, b1_in.at[plane], c_send.at[3], c_recv.at[3], (z * 2 + core, 0)
        )

    @pl.when(jnp.logical_not(owner))
    def _():
        send_bias().start()

    for dx, dy in PLANE:
        p = ((x + dx) % 4) * 4 + (y + dy) % 4
        remote(
            c1_out.at[p], c1_in.at[plane], c_send.at[0], c_recv.at[0], device(dx, dy, 0, 0)
        ).start()
    c1_in[plane] = c1_out[plane]
    act_ref[...] = (pre * sig).astype(BF16)
    for finish in pending:
        finish()
    pending.clear()
    pending.append(lambda: wait_bytes(c1_out.at[pl.ds(0, 15)], c_send.at[0]))
    pending.append(lambda: pl.when(jnp.logical_not(owner))(lambda: send_bias().wait_send()))
    wait_bytes(c1_in.at[pl.ds(0, 15)], c_recv.at[0])
    c2_in[column, 0:16] = jnp.sum(c1_in[...].astype(F32), axis=0).astype(BF16)

    def share_column(rows, start):
        piece = c2_in.at[column, pl.ds(0, rows)]
        for dz, dcore in COLUMN:
            remote(piece, piece, c_send.at[1], c_recv.at[1], device(0, 0, dz, dcore)).start()
        for finish in pending:
            finish()

    @pl.when(owner)
    def _():
        b1_in[0] = b1_out[...]
        wait_bytes(b1_in.at[pl.ds(0, 15)], c_recv.at[3])
        summed = jnp.sum(b1_in[...], axis=0)
        c2_in[column, 16:32] = jnp.concatenate([summed, jnp.zeros_like(summed)], axis=0).astype(BF16)
        share_column(32, True)
        wait_bytes(c2_in.at[pl.ds(0, 15)], c_recv.at[1])
        c3_in[0, 16:24] = jnp.sum(c2_in[:, 16:32].astype(F32), axis=0)[0:8]

    @pl.when(jnp.logical_not(owner))
    def _():
        share_column(16, True)
        wait_bytes(c2_in.at[pl.ds(0, 15), pl.ds(0, 16)], c_recv.at[1])

    pending.clear()

    @pending.append
    def _():
        pl.when(owner)(lambda: wait_bytes(c2_in.at[pl.ds(0, 15)], c_send.at[1]))
        pl.when(jnp.logical_not(owner))(
            lambda: wait_bytes(c2_in.at[pl.ds(0, 15), pl.ds(0, 16)], c_send.at[1])
        )

    c3_in[plane, 0:16] = jnp.sum(c2_in[:, 0:16].astype(F32), axis=0)

    @pl.when(owner)
    def _():
        for dx, dy in PLANE:
            remote(
                c3_in.at[0], c3_in.at[0], c_send.at[2], c_recv.at[4], device(dx, dy, 0, 0)
            ).start()
        for finish in pending:
            finish()
        wait_bytes(c3_in.at[pl.ds(0, 15), pl.ds(0, 16)], c_recv.at[2])

    @pl.when(jnp.logical_not(owner))
    def _():
        piece = c3_in.at[plane, pl.ds(0, 16)]
        for dx, dy in PLANE:
            remote(piece, piece, c_send.at[2], c_recv.at[2], device(dx, dy, 0, 0)).start()
        for finish in pending:
            finish()
        wait_bytes(c3_in.at[pl.ds(0, 14), pl.ds(0, 16)], c_recv.at[2])
        wait_bytes(c3_in.at[0], c_recv.at[4])

    pending.clear()

    @pending.append
    def _():
        pl.when(owner)(lambda: wait_bytes(c3_in.at[pl.ds(0, 15)], c_send.at[2]))
        pl.when(jnp.logical_not(owner))(
            lambda: wait_bytes(c3_in.at[pl.ds(0, 15), pl.ds(0, 16)], c_send.at[2])
        )

    wg_ref[:, 0:128] = c3_in[0:8, 0:16].reshape(128, 128)
    wg_ref[:, 128:256] = c3_in[8:16, 0:16].reshape(128, 128)
    bg_ref[:, 0:128] = c3_in[0, 16:17]
    bg_ref[:, 128:256] = c3_in[0, 17:18]

    for finish in pending:
        finish()


def hand_out(act_in, wg_in, bg_in, act_ref, wg_ref, bg_ref):
    act_ref[...] = act_in[...]
    wg_ref[...] = wg_in[...]
    bg_ref[...] = bg_in[...]


def shards(features, adj_tiles, tile_coords, tile_counts, weight, out_bias, out_grad):
    vmem = pl.BlockSpec(memory_space=pltpu.VMEM)
    dma = pltpu.SemaphoreType.DMA
    outs = (
        jax.ShapeDtypeStruct((128, 256), BF16),
        jax.ShapeDtypeStruct((128, 256), F32),
        jax.ShapeDtypeStruct((1, 256), F32),
    )
    results = pl.pallas_call(
        layer_kernel,
        name="layer",
        out_shape=outs,
        in_specs=[
            pl.BlockSpec(memory_space=pltpu.SMEM),
            vmem,
            vmem,
            pl.BlockSpec(memory_space=pl.ANY),
            vmem,
            vmem,
            vmem,
        ],
        out_specs=(vmem, vmem, vmem),
        scratch_shapes=[
            pltpu.VMEM((129, 128, 128), BF16),
            pltpu.VMEM((4, 128), jnp.int32),
            pltpu.SMEM((4, 128), jnp.int32),
            pltpu.VMEM((8, 128, 128), BF16),
            pltpu.VMEM((4, 8, 128, 128), BF16),
            pltpu.VMEM((8, 128, 128), F32),
            pltpu.VMEM((8, 128, 128), BF16),
            pltpu.VMEM((8, 128, 128), BF16),
            pltpu.VMEM((16, 16, 128), BF16),
            pltpu.VMEM((16, 16, 128), BF16),
            pltpu.VMEM((8, 128), F32),
            pltpu.VMEM((16, 8, 128), F32),
            pltpu.VMEM((16, 32, 128), BF16),
            pltpu.VMEM((16, 24, 128), F32),
            dma,
            dma,
            dma((16,)),
            dma((8,)),
            dma((8, 2)),
            dma((4,)),
            dma((4,)),
            dma,
            dma,
            dma((4,)),
            dma((5,)),
        ],
        compiler_params=pltpu.CompilerParams(
            collective_id=1, has_side_effects=True, vmem_limit_bytes=60 << 20
        ),
        cost_estimate=pl.CostEstimate(
            flops=2 * 256 * 128**3, bytes_accessed=5 << 20, transcendentals=128 * 256
        ),
    )(
        tile_counts.reshape(4),
        jnp.swapaxes(tile_coords[0, 0], 1, 2),
        features.reshape(8, 128, 128),
        adj_tiles.reshape(128, 128, 128),
        weight,
        out_bias.reshape(1, 256),
        out_grad,
    )
    activated, weight_grad, bias_grad = pl.pallas_call(
        hand_out,
        name="hand_out",
        out_shape=outs,
        in_specs=[vmem, vmem, vmem],
        out_specs=(vmem, vmem, vmem),
    )(*results)
    return activated, weight_grad, bias_grad.reshape(256)


def solution(mesh):
    placed = (
        P("row", None),
        P("row", "rep", None, None, None, None),
        P("row", "rep", None, None, None),
        P("row", "rep", None),
        P(),
        P(),
        P(("row", "rep"), None),
    )
    return jax.shard_map(
        shards,
        mesh=mesh,
        in_specs=placed,
        out_specs=(P(("row", "rep"), None), P(), P()),
        check_vma=False,
    )
```

time: 61.4 us -> 50.4 us (0.82)
  local copies, waits for them, and re-layouts: 4.91 us -> 0 us
  Pallas kernels: 53.9 us -> 49.6 us
  other arithmetic: 1.71 us -> 0 us
    pallas_call x1 -> x2, Pallas kernels: 53.9 us -> 49.6 us  [the longest x1 48 us: shards(): pl.pallas_call(layer_kernel, name='layer', out_shape=outs, in_specs=[pl.B...]
    unnamed x3 -> x0, local copies, waits for them, and re-layouts: 4.27 us -> none
    add x2 -> x0, other arithmetic: 0.77 us -> none  [the longest x1 0.77 us: slot_of_tile(): key = coords[:, :, 0] * 8 + coords[:, :, 1]]
    lt x1 -> x0, other arithmetic: 0.73 us -> none  [slot_of_tile(): live = jnp.arange(slots)[None, :] < counts[:, None]]
    add x1 -> x0, local copies, waits for them, and re-layouts: 0.65 us -> none  [slot_of_tile(): jnp.sum(jnp.where(hit, slot[:, None, :], 0), axis=-1) + sections * slots]
where the time goes in v2:
time: 50.4 us; the launch traced here: 50.2 us
  Pallas kernels  49.6 us (98%)
  between operations  0.64 us (1%)
    pallas_call x1, Pallas kernels, shards(): pl.pallas_call(layer_kernel, name='layer', out_shape=outs, in_specs=[pl.B...  48 us
    pallas_call x1, Pallas kernels, shards(): pl.pallas_call(hand_out, name='hand_out', out_shape=outs, in_specs=[vmem,...  1.59 us

profile of v2, /device:TPU:1, one launch (start us, length us, event | category | flops | bytes accessed | tf_op | source)
XLA Modules:
  0.0 50.2 jit_solution(13240241352773228925)
XLA Ops:
  0.6 48.0 %layer.1 = (bf16[128,256]{1,0:T(8,128)(2,1)}, f32[128,256]{1,0:T(8,128)}, f32[1,256]{1,0:T(1,128)}) custom-call(s32[4]{0:T(128)} %bitcast.12, s32[4,2,32]{2,1,0:T(2,128)} %bitcast.10, bf16[8,128,128]{2,1,0:T(8,128)(2,1)} %bitcast.9, bf16[128,128,128]{2,1,0:T(8,128)(2,1)} %bitcast.8, bf16[128,256]{1,0:T(8,128)(2,1)} %weight_ref.1, f32[1,256]{1,0:T(1,128)} %bitcast.11, ...), custom_call_target="tpu_custom_call" | custom-call | flops 1073741824 | bytes 5242880 | tf_op jit(solution)/shard_map/layer/pallas_call | solution.py:366
  48.6 1.6 %hand_out.1 = (bf16[128,256]{1,0:T(8,128)(2,1)}, f32[128,256]{1,0:T(8,128)}, f32[1,256]{1,0:T(1,128)}) custom-call(bf16[128,256]{1,0:T(8,128)(2,1)} %get-tuple-element.9.act_in, f32[128,256]{1,0:T(8,128)} %get-tuple-element.10.wg_in, f32[1,256]{1,0:T(1,128)} %get-tuple-element.11.bg_in), custom_call_target="tpu_custom_call" | custom-call | tf_op jit(solution)/shard_map/hand_out/pallas_call | solution.py:422

commit v3 on v2

v3 whole, which is shorter than its diff:
```python
import functools

import jax
import jax.numpy as jnp
from jax import lax
from jax.experimental import pallas as pl
from jax.experimental.pallas import tpu as pltpu
from jax.sharding import PartitionSpec as P

MESH = pl.DeviceIdType.MESH
F32 = jnp.float32
BF16 = jnp.bfloat16

PLANE = sorted(
    [(dx, dy) for dx in range(4) for dy in range(4) if (dx, dy) != (0, 0)],
    key=lambda o: -(min(o[0], 4 - o[0]) + min(o[1], 4 - o[1])),
)
ALONG_Z = [4, 3, 5, 2, 6, 1, 7]
GREETED = [(0, 0, dz, dcore) for dz in (2, 6, 1, 7) for dcore in (0, 1)] + [(0, 0, 0, 1)]
GREETED += [(d, 0, 0, 0) for d in (2, 1, 3)] + [(0, d, 0, 0) for d in (2, 1, 3)]


def layer_kernel(
    counts_hbm,
    coords_hbm,
    feat_hbm,
    adj_hbm,
    weight_hbm,
    bias_hbm,
    cot_hbm,
    act_ref,
    wg_ref,
    bg_ref,
    counts_ref,
    coords_ref,
    weight_ref,
    bias_ref,
    cot_ref,
    tiles,
    slot_rows,
    slots,
    held,
    feats,
    acc,
    part_out,
    part_in,
    c1_out,
    c1_in,
    b1_out,
    b1_in,
    core_io,
    c2_in,
    c3_in,
    load_sem,
    slot_sem,
    a1_send,
    a1_recv,
    a2_send,
    a2_recv,
    a3_send,
    a3_recv,
    b_send,
    b_recv,
    c_send,
    c_recv,
):
    row = lax.axis_index("row")
    rep = lax.axis_index("rep")
    xh, z, core = row // 16, (row // 2) % 8, row % 2
    xl, y = rep // 4, rep % 4
    x = xh * 2 + xl
    plane = x * 4 + y
    live = tiles.shape[0] - 1

    def device(dx, dy, dz, dcore):
        x2, y2, z2, c2 = (x + dx) % 4, (y + dy) % 4, (z + dz) % 8, (core + dcore) % 2
        return (x2 // 2) * 16 + z2 * 2 + c2, (x2 % 2) * 4 + y2

    def remote(src, dst, send, recv, target):
        return pltpu.make_async_remote_copy(
            src_ref=src,
            dst_ref=dst,
            send_sem=send,
            recv_sem=recv,
            device_id=target,
            device_id_type=MESH,
        )

    def wait_bytes(ref, sem):
        pltpu.make_async_copy(ref, ref, sem).wait()

    barrier = pltpu.get_barrier_semaphore()
    for offset in GREETED:
        pl.semaphore_signal(barrier, inc=1, device_id=device(*offset), device_id_type=MESH)

    pending = []
    loads = [
        pltpu.make_async_copy(src, dst, load_sem.at[n])
        for n, (src, dst) in enumerate(
            [
                (counts_hbm, counts_ref),
                (coords_hbm, coords_ref),
                (adj_hbm, tiles.at[pl.ds(0, live)]),
                (weight_hbm, weight_ref),
                (bias_hbm, bias_ref),
                (cot_hbm, cot_ref),
            ]
        )
    ]
    for load in loads:
        load.start()
    tile_copy = loads[2]

    tiles[live] = jnp.zeros(tiles.shape[1:], BF16)
    lane = lax.broadcasted_iota(jnp.int32, (64, 32), 1)
    sub = lax.broadcasted_iota(jnp.int32, (64, 32), 0)
    wide_lane = lax.broadcasted_iota(jnp.int32, (64, 128), 1)
    wide_sub = lax.broadcasted_iota(jnp.int32, (64, 128), 0)
    loads[0].wait()
    loads[1].wait()
    for t in range(4):
        key = coords_ref[t, 0:1, :] * 8 + coords_ref[t, 1:2, :]
        hit = jnp.logical_and(key == sub, lane < counts_ref[0:1, t : t + 1])
        found = jnp.sum(jnp.where(hit, lane + (t * 32 + 1), 0), axis=1, keepdims=True)
        turned = jnp.sum(jnp.where(wide_lane == wide_sub, found, 0), axis=0, keepdims=True)
        slot_rows[t : t + 1, :] = jnp.where(turned == 0, live, turned - 1)
    slot_copy = pltpu.make_async_copy(slot_rows, slots, slot_sem)
    slot_copy.start()

    b1_out[...] = jnp.zeros_like(b1_out)
    part_in[rep] = jnp.zeros(part_in.shape[1:], BF16)
    pl.semaphore_wait(barrier, len(GREETED))

    even = z % 2 == y // 2
    source = jnp.logical_and(even, core == y % 2)

    def along_z(n, dz, to_core):
        return remote(
            feat_hbm.at[pl.ds(xl * 4 + to_core * 2, 2)],
            held.at[z],
            a1_send.at[n],
            a1_recv.at[z],
            (xh * 16 + ((z + dz) % 8) * 2 + to_core, rep),
        )

    def own_quarter():
        return pltpu.make_async_copy(
            feat_hbm.at[pl.ds(xl * 4 + core * 2, 2)], held.at[z], a1_recv.at[z]
        )

    def to_column(start):
        for n, dz in enumerate((2, 6, 1, 7)):
            for to_core in (0, 1):
                copy = along_z(2 * n + to_core, dz, to_core)
                copy.start() if start else copy.wait_send()
        copy = along_z(8, 0, 1 - core)
        copy.start() if start else copy.wait_send()

    pl.when(source)(lambda: (own_quarter().start(), to_column(True)) and None)
    pending.append(lambda: pl.when(source)(lambda: to_column(False)))

    def pass_along(n, dz, to, first, count):
        src = (z + dz) % 8
        piece = held.at[src, pl.ds(first, count)]
        return remote(piece, piece, a1_send.at[9 + n], a1_recv.at[src], device(0, 0, to, 0))

    relays = [(0, 2, -2, 0, 1), (1, 2, -1, 0, 2), (2, 6, 2, 1, 1), (3, 6, 1, 0, 2)]
    pending.append(
        lambda: pl.when(even)(lambda: [pass_along(*r).wait_send() for r in relays] and None)
    )

    def to_user(dz, target_xh, start):
        src = (z + dz) % 8
        user_xl = (src % 4) // 2
        mine = jnp.logical_and(user_xl == xl, xh == target_xh)
        section = xh * 2 + src // 4
        piece = held.at[src]
        place = feats.at[section, xl, core]

        @pl.when(jnp.logical_not(mine))
        def _():
            copy = remote(
                piece,
                place,
                a2_send.at[dz, target_xh],
                a2_recv.at[section],
                (target_xh * 16 + z * 2 + core, user_xl * 4 + y),
            )
            copy.start() if start else copy.wait_send()

        if start:

            @pl.when(mine)
            def _():
                pltpu.make_async_copy(piece, place, a2_recv.at[section]).start()

    def to_users(dz, start=True):
        for target_xh in (0, 1):
            to_user(dz, target_xh, start)

    def wait_piece(dz):
        src = (z + dz) % 8
        wait_bytes(held.at[src], a1_recv.at[src])

    @pl.when(even)
    def _():
        wait_piece(0)
        to_users(0)
        wait_piece(2)
        for r in relays[:2]:
            pass_along(*r).start()
        wait_piece(6)
        for r in relays[2:]:
            pass_along(*r).start()
        to_users(2)
        to_users(6)
        wait_piece(4)
        to_users(4)

    @pl.when(jnp.logical_not(even))
    def _():
        for dz in (1, 7, 3, 5):
            wait_piece(dz)
            to_users(dz)

    pending.append(lambda: pl.when(even)(lambda: [to_users(d, False) for d in (0, 2, 6, 4)] and None))
    pending.append(
        lambda: pl.when(jnp.logical_not(even))(
            lambda: [to_users(d, False) for d in (1, 7, 3, 5)] and None
        )
    )

    nearer = ((rep // 2 - z + 10) % 8) // 5
    order = [xh * 2 + nearer, 2 - xh * 2 + nearer, xh * 2 + 1 - nearer, 3 - xh * 2 - nearer]

    def pass_on(section):
        piece = feats.at[section, pl.ds(0, 2), core]
        wait_bytes(piece, a2_recv.at[section])
        launch(remote(piece, piece, a3_send.at[section], a3_recv.at[section], device(0, 0, 0, 1)))

    def complete(section):
        wait_bytes(feats.at[section, pl.ds(0, 2), 1 - core], a3_recv.at[section])

    def launch(copy):
        copy.start()
        pending.append(copy.wait_send)

    def products(r, sections, half):
        left, right = [], []
        for section in sections:
            for k in range(4):
                q = (k // 2) * 4 + half * 2 + k % 2
                left.append(tiles[slots[section, r * 8 + q]])
            right.append(feats[section, :, half].reshape(4 * 128, 128))
        return jnp.dot(
            jnp.concatenate(left, axis=1),
            jnp.concatenate(right, axis=0),
            preferred_element_type=F32,
        )

    def add_products(sections, half, first):
        for r in range(8):
            term = products(r, sections, half)
            acc[r] = term if first else acc[r] + term

    near, far = order[:2], order[2:]
    tile_copy.wait()
    slot_copy.wait()
    pass_on(near[0])
    pass_on(near[1])
    add_products(near, core, True)
    complete(near[0])
    complete(near[1])
    add_products(near, 1 - core, False)
    pass_on(far[0])
    pass_on(far[1])
    add_products(far, core, False)
    complete(far[0])
    complete(far[1])

    for i, k in enumerate((2, 1, 3, 0, 2, 1, 3, 0)):
        r = ((xl + 1 - i // 4) % 2) * 4 + (y + k) % 4
        total = acc[r] + products(r, far, 1 - core)
        if i < 7:
            part_out[r] = total.astype(BF16)
            remote(part_out.at[r], part_in.at[rep], b_send, b_recv, (row, r)).start()

    for finish in pending:
        finish()
    pending.clear()
    pending.append(lambda: wait_bytes(part_out.at[pl.ds(0, 7)], b_send))
    wait_bytes(part_in.at[pl.ds(0, 7)], b_recv)
    for s in range(8):
        total = total + part_in[s].astype(F32)

    for load in loads[3:]:
        load.wait()
    aggregated = total.astype(BF16)
    pre = jnp.dot(aggregated, weight_ref[...], preferred_element_type=F32) + bias_ref[...]
    sig = jax.nn.sigmoid(pre)
    grad = (cot_ref[...].astype(F32) * sig * (1.0 + pre * (1.0 - sig))).astype(BF16)
    weight_part = lax.dot_general(
        aggregated, grad, (((0,), (0,)), ((), ())), preferred_element_type=F32
    )
    bias_part = jnp.sum(grad.astype(F32), axis=0, keepdims=True)

    owner = plane == 0
    c1_out[0:8] = weight_part[:, 0:128].astype(BF16).reshape(8, 16, 128)
    c1_out[8:16] = weight_part[:, 128:256].astype(BF16).reshape(8, 16, 128)
    b1_out[0:1, :] = bias_part[:, 0:128]
    b1_out[1:2, :] = bias_part[:, 128:256]

    def send_bias():
        return remote(
            b1_out, b1_in.at[plane], c_send.at[3], c_recv.at[3], (z * 2 + core, 0)
        )

    @pl.when(jnp.logical_not(owner))
    def _():
        send_bias().start()

    for dx, dy in PLANE:
        p = ((x + dx) % 4) * 4 + (y + dy) % 4
        remote(
            c1_out.at[p], c1_in.at[plane], c_send.at[0], c_recv.at[0], device(dx, dy, 0, 0)
        ).start()
    c1_in[plane] = c1_out[plane]
    act_ref[...] = (pre * sig).astype(BF16)
    for finish in pending:
        finish()
    pending.clear()
    pending.append(lambda: wait_bytes(c1_out.at[pl.ds(0, 15)], c_send.at[0]))
    pending.append(lambda: pl.when(jnp.logical_not(owner))(lambda: send_bias().wait_send()))
    wait_bytes(c1_in.at[pl.ds(0, 15)], c_recv.at[0])
    core_io[core, 0:16] = jnp.sum(c1_in[...].astype(F32), axis=0)

    @pl.when(owner)
    def _():
        b1_in[0] = b1_out[...]
        wait_bytes(b1_in.at[pl.ds(0, 15)], c_recv.at[3])
        core_io[core, 16:24] = jnp.sum(b1_in[...], axis=0)

    def to_other_core():
        piece = core_io.at[core]
        return remote(piece, piece, c_send.at[4], c_recv.at[5], device(0, 0, 0, 1))

    to_other_core().start()
    wait_bytes(core_io.at[1 - core], c_recv.at[5])
    c2_in[z, 0:16] = (core_io[0, 0:16] + core_io[1, 0:16]).astype(BF16)

    def share_column(rows):
        piece = c2_in.at[z, pl.ds(0, rows)]
        for dz in ALONG_Z:
            remote(piece, piece, c_send.at[1], c_recv.at[1], device(0, 0, dz, 0)).start()
        for finish in pending:
            finish()
        wait_bytes(c2_in.at[pl.ds(0, 7), pl.ds(0, rows)], c_recv.at[1])

    @pl.when(owner)
    def _():
        both = core_io[0, 16:24] + core_io[1, 16:24]
        c2_in[z, 16:32] = jnp.concatenate([both, jnp.zeros_like(both)], axis=0).astype(BF16)
        share_column(32)
        c3_in[0, 16:24] = jnp.sum(c2_in[:, 16:32].astype(F32), axis=0)[0:8]

    pl.when(jnp.logical_not(owner))(lambda: share_column(16))
    pending.clear()

    @pending.append
    def _():
        to_other_core().wait_send()
        pl.when(owner)(lambda: wait_bytes(c2_in.at[pl.ds(0, 7)], c_send.at[1]))
        pl.when(jnp.logical_not(owner))(
            lambda: wait_bytes(c2_in.at[pl.ds(0, 7), pl.ds(0, 16)], c_send.at[1])
        )

    c3_in[plane, 0:16] = jnp.sum(c2_in[:, 0:16].astype(F32), axis=0)

    @pl.when(owner)
    def _():
        for dx, dy in PLANE:
            remote(
                c3_in.at[0], c3_in.at[0], c_send.at[2], c_recv.at[4], device(dx, dy, 0, 0)
            ).start()
        for finish in pending:
            finish()
        wait_bytes(c3_in.at[pl.ds(0, 15), pl.ds(0, 16)], c_recv.at[2])

    @pl.when(jnp.logical_not(owner))
    def _():
        piece = c3_in.at[plane, pl.ds(0, 16)]
        for dx, dy in PLANE:
            remote(piece, piece, c_send.at[2], c_recv.at[2], device(dx, dy, 0, 0)).start()
        for finish in pending:
            finish()
        wait_bytes(c3_in.at[pl.ds(0, 14), pl.ds(0, 16)], c_recv.at[2])
        wait_bytes(c3_in.at[0], c_recv.at[4])

    pending.clear()

    @pending.append
    def _():
        pl.when(owner)(lambda: wait_bytes(c3_in.at[pl.ds(0, 15)], c_send.at[2]))
        pl.when(jnp.logical_not(owner))(
            lambda: wait_bytes(c3_in.at[pl.ds(0, 15), pl.ds(0, 16)], c_send.at[2])
        )

    wg_ref[:, 0:128] = c3_in[0:8, 0:16].reshape(128, 128)
    wg_ref[:, 128:256] = c3_in[8:16, 0:16].reshape(128, 128)
    bg_ref[:, 0:128] = c3_in[0, 16:17]
    bg_ref[:, 128:256] = c3_in[0, 17:18]

    for finish in pending:
        finish()


def hand_out(act_in, wg_in, bg_in, act_ref, wg_ref, bg_ref):
    act_ref[...] = act_in[...]
    wg_ref[...] = wg_in[...]
    bg_ref[...] = bg_in[...]


def shards(features, adj_tiles, tile_coords, tile_counts, weight, out_bias, out_grad):
    vmem = pl.BlockSpec(memory_space=pltpu.VMEM)
    dma = pltpu.SemaphoreType.DMA
    outs = (
        jax.ShapeDtypeStruct((128, 256), BF16),
        jax.ShapeDtypeStruct((128, 256), F32),
        jax.ShapeDtypeStruct((1, 256), F32),
    )
    results = pl.pallas_call(
        layer_kernel,
        name="layer",
        out_shape=outs,
        in_specs=[pl.BlockSpec(memory_space=pl.ANY)] * 7,
        out_specs=(vmem, vmem, vmem),
        scratch_shapes=[
            pltpu.VMEM((1, 4), jnp.int32),
            pltpu.VMEM((4, 2, 32), jnp.int32),
            pltpu.VMEM((128, 256), BF16),
            pltpu.VMEM((1, 256), F32),
            pltpu.VMEM((128, 256), BF16),
            pltpu.VMEM((129, 128, 128), BF16),
            pltpu.VMEM((4, 128), jnp.int32),
            pltpu.SMEM((4, 128), jnp.int32),
            pltpu.VMEM((8, 2, 128, 128), BF16),
            pltpu.VMEM((4, 2, 2, 2, 128, 128), BF16),
            pltpu.VMEM((8, 128, 128), F32),
            pltpu.VMEM((8, 128, 128), BF16),
            pltpu.VMEM((8, 128, 128), BF16),
            pltpu.VMEM((16, 16, 128), BF16),
            pltpu.VMEM((16, 16, 128), BF16),
            pltpu.VMEM((8, 128), F32),
            pltpu.VMEM((16, 8, 128), F32),
            pltpu.VMEM((2, 24, 128), F32),
            pltpu.VMEM((8, 32, 128), BF16),
            pltpu.VMEM((16, 24, 128), F32),
            dma((6,)),
            dma,
            dma((16,)),
            dma((8,)),
            dma((8, 2)),
            dma((4,)),
            dma((4,)),
            dma((4,)),
            dma,
            dma,
            dma((5,)),
            dma((6,)),
        ],
        compiler_params=pltpu.CompilerParams(
            collective_id=1, has_side_effects=True, vmem_limit_bytes=60 << 20
        ),
        cost_estimate=pl.CostEstimate(
            flops=2 * 256 * 128**3, bytes_accessed=5 << 20, transcendentals=128 * 256
        ),
    )(
        tile_counts.reshape(1, 4),
        jnp.swapaxes(tile_coords[0, 0], 1, 2),
        features.reshape(8, 128, 128),
        adj_tiles.reshape(128, 128, 128),
        weight,
        out_bias.reshape(1, 256),
        out_grad,
    )
    activated, weight_grad, bias_grad = pl.pallas_call(
        hand_out,
        name="hand_out",
        out_shape=outs,
        in_specs=[vmem, vmem, vmem],
        out_specs=(vmem, vmem, vmem),
    )(*results)
    return activated, weight_grad, bias_grad.reshape(256)


def solution(mesh):
    placed = (
        P("row", None),
        P("row", "rep", None, None, None, None),
        P("row", "rep", None, None, None),
        P("row", "rep", None),
        P(),
        P(),
        P(("row", "rep"), None),
    )
    return jax.shard_map(
        shards,
        mesh=mesh,
        in_specs=placed,
        out_specs=(P(("row", "rep"), None), P(), P()),
        check_vma=False,
    )
```

time: 50.4 us -> 49.2 us (0.976)
  Pallas kernels: 49.6 us -> 48.4 us
    pallas_call x1, Pallas kernels: 48 us -> 46.8 us  [shards(): pl.pallas_call(layer_kernel, name='layer', out_shape=outs, in_specs=[pl.B...]
where the time goes in v3:
time: 49.2 us; the launch traced here: 49 us
  Pallas kernels  48.4 us (98%)
  between operations  0.64 us (1%)
    pallas_call x1, Pallas kernels, shards(): pl.pallas_call(layer_kernel, name='layer', out_shape=outs, in_specs=[pl.B...  46.8 us
    pallas_call x1, Pallas kernels, shards(): pl.pallas_call(hand_out, name='hand_out', out_shape=outs, in_specs=[vmem,...  1.59 us

profile of v3, /device:TPU:1, one launch (start us, length us, event | category | flops | bytes accessed | tf_op | source)
XLA Modules:
  0.0 49.0 jit_solution(61021824160244061)
XLA Ops:
  0.6 46.8 %layer.1 = (bf16[128,256]{1,0:T(8,128)(2,1)}, f32[128,256]{1,0:T(8,128)}, f32[1,256]{1,0:T(1,128)}) custom-call(s32[1,4]{1,0:T(1,128)} %bitcast.12, s32[4,2,32]{2,1,0:T(2,128)} %bitcast.10, bf16[8,128,128]{2,1,0:T(8,128)(2,1)} %bitcast.9, bf16[128,128,128]{2,1,0:T(8,128)(2,1)} %bitcast.8, bf16[128,256]{1,0:T(8,128)(2,1)} %weight_hbm.1, f32[1,256]{1,0:T(1,128)} %bitcast.11, ...), custom_call_target="tpu_custom_call" | custom-call | flops 1073741824 | bytes 5242880 | tf_op jit(solution)/shard_map/layer/pallas_call | solution.py:431
  47.4 1.6 %hand_out.1 = (bf16[128,256]{1,0:T(8,128)(2,1)}, f32[128,256]{1,0:T(8,128)}, f32[1,256]{1,0:T(1,128)}) custom-call(bf16[128,256]{1,0:T(8,128)(2,1)} %get-tuple-element.9.act_in, f32[128,256]{1,0:T(8,128)} %get-tuple-element.10.wg_in, f32[1,256]{1,0:T(1,128)} %get-tuple-element.11.bg_in), custom_call_target="tpu_custom_call" | custom-call | tf_op jit(solution)/shard_map/hand_out/pallas_call | solution.py:486

commit v4 on v3

v4 whole, which is shorter than its diff:
```python
import functools

import jax
import jax.numpy as jnp
from jax import lax
from jax.experimental import pallas as pl
from jax.experimental.pallas import tpu as pltpu
from jax.sharding import PartitionSpec as P

MESH = pl.DeviceIdType.MESH
F32 = jnp.float32
BF16 = jnp.bfloat16

PLANE = sorted(
    [(dx, dy) for dx in range(4) for dy in range(4) if (dx, dy) != (0, 0)],
    key=lambda o: -(min(o[0], 4 - o[0]) + min(o[1], 4 - o[1])),
)
ALONG_Z = [4, 3, 5, 2, 6, 1, 7]
GREETED = [(0, 0, 0, 1)] + [(d, 0, 0, 0) for d in (2, 1, 3)] + [(0, d, 0, 0) for d in (2, 1, 3)]


def layer_kernel(
    counts_hbm,
    coords_hbm,
    feat_hbm,
    adj_hbm,
    weight_hbm,
    bias_hbm,
    cot_hbm,
    act_ref,
    wg_ref,
    bg_ref,
    counts_ref,
    coords_ref,
    weight_ref,
    bias_ref,
    cot_ref,
    tiles,
    slot_rows,
    slots,
    held,
    feats,
    acc,
    part_out,
    part_in,
    c1_out,
    c1_in,
    b1_out,
    b1_in,
    c2_in,
    c3_in,
    load_sem,
    slot_sem,
    a1_send,
    a1_recv,
    a2_send,
    a2_recv,
    a3_send,
    a3_recv,
    b_send,
    b_recv,
    c_send,
    c_recv,
):
    row = lax.axis_index("row")
    rep = lax.axis_index("rep")
    xh, z, core = row // 16, (row // 2) % 8, row % 2
    xl, y = rep // 4, rep % 4
    x = xh * 2 + xl
    plane = x * 4 + y
    live = tiles.shape[0] - 1

    def device(dx, dy, dz, dcore):
        x2, y2, z2, c2 = (x + dx) % 4, (y + dy) % 4, (z + dz) % 8, (core + dcore) % 2
        return (x2 // 2) * 16 + z2 * 2 + c2, (x2 % 2) * 4 + y2

    def remote(src, dst, send, recv, target):
        return pltpu.make_async_remote_copy(
            src_ref=src,
            dst_ref=dst,
            send_sem=send,
            recv_sem=recv,
            device_id=target,
            device_id_type=MESH,
        )

    def wait_bytes(ref, sem):
        pltpu.make_async_copy(ref, ref, sem).wait()

    barrier = pltpu.get_barrier_semaphore()
    odd_z = (z + y // 2) % 2
    other_core = (core + y) % 2

    def greet(*offset):
        pl.semaphore_signal(barrier, inc=1, device_id=device(*offset), device_id_type=MESH)

    greet(0, 0, 2 - odd_z, 0)
    greet(0, 0, 6 + odd_z, 0)

    @pl.when(other_core == 1)
    def _():
        greet(0, 0, 2 - odd_z, 1)
        greet(0, 0, 6 + odd_z, 1)

    for offset in GREETED:
        greet(*offset)

    pending = []
    loads = [
        pltpu.make_async_copy(src, dst, load_sem.at[n])
        for n, (src, dst) in enumerate(
            [
                (counts_hbm, counts_ref),
                (coords_hbm, coords_ref),
                (adj_hbm, tiles.at[pl.ds(0, live)]),
                (weight_hbm, weight_ref),
                (bias_hbm, bias_ref),
                (cot_hbm, cot_ref),
            ]
        )
    ]
    tile_copy = loads[2]
    for load in loads:
        if load is not tile_copy:
            load.start()

    tiles[live] = jnp.zeros(tiles.shape[1:], BF16)
    lane = lax.broadcasted_iota(jnp.int32, (64, 32), 1)
    sub = lax.broadcasted_iota(jnp.int32, (64, 32), 0)
    wide_lane = lax.broadcasted_iota(jnp.int32, (64, 128), 1)
    wide_sub = lax.broadcasted_iota(jnp.int32, (64, 128), 0)
    loads[0].wait()
    loads[1].wait()
    for t in range(4):
        key = coords_ref[t, 0:1, :] * 8 + coords_ref[t, 1:2, :]
        hit = jnp.logical_and(key == sub, lane < counts_ref[0:1, t : t + 1])
        found = jnp.sum(jnp.where(hit, lane + (t * 32 + 1), 0), axis=1, keepdims=True)
        turned = jnp.sum(jnp.where(wide_lane == wide_sub, found, 0), axis=0, keepdims=True)
        slot_rows[t : t + 1, :] = jnp.where(turned == 0, live, turned - 1)
    slot_copy = pltpu.make_async_copy(slot_rows, slots, slot_sem)
    slot_copy.start()

    b1_out[...] = jnp.zeros_like(b1_out)
    acc[...] = jnp.zeros_like(acc)
    part_in[rep] = jnp.zeros(part_in.shape[1:], BF16)
    pl.semaphore_wait(barrier, len(GREETED) + (1 - odd_z) * (8 - 4 * other_core))

    even = z % 2 == y // 2
    source = jnp.logical_and(even, core == y % 2)

    def along_z(n, dz, to_core, first=0, count=2):
        return remote(
            feat_hbm.at[pl.ds(xl * 4 + to_core * 2 + first, count)],
            held.at[z, pl.ds(first, count)],
            a1_send.at[n],
            a1_recv.at[z, first],
            (xh * 16 + ((z + dz) % 8) * 2 + to_core, rep),
        )

    def own_quarter():
        return pltpu.make_async_copy(
            feat_hbm.at[pl.ds(xl * 4 + core * 2, 2)], held.at[z], a1_recv.at[z, 0]
        )

    def to_column(start):
        parts = [(2, 1, 1), (6, 0, 1), (2, 0, 1), (6, 1, 1), (1, 0, 2), (7, 0, 2)]
        copies = [
            along_z(2 * n + to_core, dz, to_core, first, count)
            for n, (dz, first, count) in enumerate(parts)
            for to_core in (0, 1)
        ]
        for copy in copies + [along_z(12, 0, 1 - core)]:
            copy.start() if start else copy.wait_send()

    pl.when(source)(lambda: (own_quarter().start(), to_column(True)) and None)
    tile_copy.start()
    pending.append(lambda: pl.when(source)(lambda: to_column(False)))

    def pass_along(dz, half, start):
        src = (z + dz) % 8
        piece = held.at[src, pl.ds(half, 1)]
        side = 1 if dz == 6 else -1
        for n, far in enumerate((1, 2)):
            if far == 1 or half == (dz == 6):
                send = a1_send.at[13 + (dz // 4) * 4 + half * 2 + n]
                copy = remote(piece, piece, send, a1_recv.at[src, half], device(0, 0, side * far, 0))
                copy.start() if start else copy.wait_send()

    def to_users(dz, first, count, start=True):
        src = (z + dz) % 8
        user_xl = (src % 4) // 2
        section = xh * 2 + src // 4
        piece = held.at[src, pl.ds(first, count)]
        place = feats.at[section, xl, core, pl.ds(first, count)]

        def send(n, target_xh):
            copy = remote(
                piece,
                place,
                a2_send.at[dz, n, first],
                a2_recv.at[section],
                (target_xh * 16 + z * 2 + core, user_xl * 4 + y),
            )
            copy.start() if start else copy.wait_send()

        send(0, 1 - xh)
        pl.when(user_xl != xl)(lambda: send(1, xh))
        if start:

            @pl.when(user_xl == xl)
            def _():
                pltpu.make_async_copy(piece, place, a2_recv.at[section]).start()

    def wait_piece(dz, first, count):
        src = (z + dz) % 8
        wait_bytes(held.at[src, pl.ds(first, count)], a1_recv.at[src, first])

    even_parts = [(0, 0, 2), (2, 0, 1), (6, 1, 1), (2, 1, 1), (6, 0, 1), (4, 0, 1), (4, 1, 1)]
    odd_parts = [(1, 0, 2), (7, 0, 2), (3, 0, 1), (5, 1, 1), (3, 1, 1), (5, 0, 1)]

    @pl.when(even)
    def _():
        for dz, first, count in even_parts:
            wait_piece(dz, first, count)
            if dz in (2, 6):
                pass_along(dz, first, True)
            to_users(dz, first, count)

    @pl.when(jnp.logical_not(even))
    def _():
        for dz, first, count in odd_parts:
            wait_piece(dz, first, count)
            to_users(dz, first, count)

    def drain_even():
        for part in even_parts:
            if part[0] in (2, 6):
                pass_along(part[0], part[1], False)
            to_users(*part, start=False)

    def drain_odd():
        for part in odd_parts:
            to_users(*part, start=False)

    pending.append(lambda: pl.when(even)(drain_even))
    pending.append(lambda: pl.when(jnp.logical_not(even))(drain_odd))

    nearer = ((rep // 2 - z + 10) % 8) // 5
    def pair(turn):
        th = (turn // 2 + nearer) % 2
        return xh * 2 + th, (1 - xh) * 2 + th

    def pass_on(section, start):
        piece = feats.at[section, pl.ds(0, 2), core]
        copy = remote(
            piece, piece, a3_send.at[section], a3_recv.at[section], device(0, 0, 0, 1)
        )
        if start:
            wait_bytes(piece, a2_recv.at[section])
            copy.start()
        else:
            copy.wait_send()

    def complete(section):
        wait_bytes(feats.at[section, pl.ds(0, 2), 1 - core], a3_recv.at[section])

    def products(r, sections, half):
        left, right = [], []
        for section in sections:
            for k in range(4):
                q = (k // 2) * 4 + half * 2 + k % 2
                left.append(tiles[slots[section, r * 8 + q]])
            right.append(feats[section, :, half].reshape(4 * 128, 128))
        return jnp.dot(
            jnp.concatenate(left, axis=1),
            jnp.concatenate(right, axis=0),
            preferred_element_type=F32,
        )

    tile_copy.wait()
    slot_copy.wait()
    tile_rows = [
        ((xl + 1 - i // 4) % 2) * 4 + (y + k) % 4 for i, k in enumerate((2, 1, 3, 0, 2, 1, 3, 0))
    ]

    def add_products(turn, carry):
        sections = pair(turn)

        @pl.when(turn % 2 == 0)
        def _():
            for section in sections:
                pass_on(section, True)

        @pl.when(turn % 2 == 1)
        def _():
            for section in sections:
                complete(section)

        for r in tile_rows:
            total = acc[r] + products(r, sections, (core + turn) % 2)
            acc[r] = total
        return carry

    pending.append(lambda: [pass_on(t, False) for t in range(4)])
    lax.fori_loop(0, 3, add_products, 0)
    for section in pair(3):
        complete(section)
    for r in tile_rows:
        total = acc[r] + products(r, pair(3), 1 - core)
        if r is not tile_rows[7]:
            part_out[r] = total.astype(BF16)
            remote(part_out.at[r], part_in.at[rep], b_send, b_recv, (row, r)).start()

    for finish in pending:
        finish()
    pending.clear()
    pending.append(lambda: wait_bytes(part_out.at[pl.ds(0, 7)], b_send))
    wait_bytes(part_in.at[pl.ds(0, 7)], b_recv)
    for s in range(8):
        total = total + part_in[s].astype(F32)

    for load in loads[3:]:
        load.wait()
    aggregated = total.astype(BF16)
    pre = jnp.dot(aggregated, weight_ref[...], preferred_element_type=F32) + bias_ref[...]
    sig = jax.nn.sigmoid(pre)
    grad = (cot_ref[...].astype(F32) * sig * (1.0 + pre * (1.0 - sig))).astype(BF16)
    weight_part = lax.dot_general(
        aggregated, grad, (((0,), (0,)), ((), ())), preferred_element_type=F32
    )
    bias_part = jnp.sum(grad.astype(F32), axis=0, keepdims=True)

    first = plane == 0
    active = core == y % 2
    owner = jnp.logical_and(first, active)
    c1_out[0:8] = weight_part[:, 0:128].astype(BF16).reshape(8, 16, 128)
    c1_out[8:16] = weight_part[:, 128:256].astype(BF16).reshape(8, 16, 128)
    b1_out[0:1, :] = bias_part[:, 0:128]
    b1_out[1:2, :] = bias_part[:, 128:256]

    def send_bias():
        place = b1_in.at[plane * 2 + core]
        return remote(b1_out, place, c_send.at[3], c_recv.at[3], (z * 2, 0))

    def send_piece(dx, dy):
        x2, y2 = (x + dx) % 4, (y + dy) % 4
        target = (x2 // 2) * 16 + z * 2 + y2 % 2, (x2 % 2) * 4 + y2
        place = c1_in.at[plane * 2 + core]
        return remote(c1_out.at[x2 * 4 + y2], place, c_send.at[0], c_recv.at[0], target)

    @pl.when(jnp.logical_not(owner))
    def _():
        send_bias().start()

    for dx, dy in PLANE:
        send_piece(dx, dy).start()

    @pl.when(active)
    def _():
        c1_in[plane * 2 + core] = c1_out[plane]

    @pl.when(jnp.logical_not(active))
    def _():
        send_piece(0, 0).start()

    act_ref[...] = (pre * sig).astype(BF16)
    for finish in pending:
        finish()
    pending.clear()

    @pending.append
    def _():
        pl.when(jnp.logical_not(owner))(lambda: send_bias().wait_send())
        pl.when(active)(lambda: wait_bytes(c1_out.at[pl.ds(0, 15)], c_send.at[0]))
        pl.when(jnp.logical_not(active))(lambda: wait_bytes(c1_out, c_send.at[0]))

    pl.when(active)(lambda: wait_bytes(c1_in.at[pl.ds(0, 31)], c_recv.at[0]))

    def share_column(rows, start):
        piece = c2_in.at[z, pl.ds(0, rows)]
        for dz in ALONG_Z + [0]:
            for dcore in (0, 1):
                if dz or dcore:
                    copy = remote(
                        piece, piece, c_send.at[1], c_recv.at[1], device(0, 0, dz, dcore)
                    )
                    copy.start()

    def column_bytes(count, sem):
        pl.when(first)(lambda: wait_bytes(c2_in.at[pl.ds(0, count)], sem))
        pl.when(jnp.logical_not(first))(
            lambda: wait_bytes(c2_in.at[pl.ds(0, count), pl.ds(0, 16)], sem)
        )

    @pl.when(active)
    def _():
        c2_in[z, 0:16] = jnp.sum(c1_in[...].astype(F32), axis=0).astype(BF16)

        @pl.when(first)
        def _():
            b1_in[0] = b1_out[...]
            wait_bytes(b1_in.at[pl.ds(0, 31)], c_recv.at[3])
            both = jnp.sum(b1_in[...], axis=0)
            c2_in[z, 16:32] = jnp.concatenate([both, jnp.zeros_like(both)], axis=0).astype(BF16)
            share_column(32, True)

        pl.when(jnp.logical_not(first))(lambda: share_column(16, True))

    for finish in pending:
        finish()
    pending.clear()
    pl.when(active)(lambda: column_bytes(7, c_recv.at[1]))
    pl.when(jnp.logical_not(active))(lambda: column_bytes(8, c_recv.at[1]))

    @pl.when(first)
    def _():
        c3_in[0, 16:32] = jnp.sum(c2_in[:, 16:32].astype(F32), axis=0).astype(BF16)

    @pending.append
    def _():
        pl.when(active)(lambda: (column_bytes(8, c_send.at[1]), column_bytes(7, c_send.at[1])) and None)

    c3_in[plane, 0:16] = jnp.sum(c2_in[:, 0:16].astype(F32), axis=0).astype(BF16)

    @pl.when(first)
    def _():
        for dx, dy in PLANE:
            remote(
                c3_in.at[0], c3_in.at[0], c_send.at[2], c_recv.at[4], device(dx, dy, 0, 0)
            ).start()
        for finish in pending:
            finish()
        wait_bytes(c3_in.at[pl.ds(0, 15), pl.ds(0, 16)], c_recv.at[2])

    @pl.when(jnp.logical_not(first))
    def _():
        piece = c3_in.at[plane, pl.ds(0, 16)]
        for dx, dy in PLANE:
            remote(piece, piece, c_send.at[2], c_recv.at[2], device(dx, dy, 0, 0)).start()
        for finish in pending:
            finish()
        wait_bytes(c3_in.at[pl.ds(0, 14), pl.ds(0, 16)], c_recv.at[2])
        wait_bytes(c3_in.at[0], c_recv.at[4])

    pending.clear()

    @pending.append
    def _():
        pl.when(first)(lambda: wait_bytes(c3_in.at[pl.ds(0, 15)], c_send.at[2]))
        pl.when(jnp.logical_not(first))(
            lambda: wait_bytes(c3_in.at[pl.ds(0, 15), pl.ds(0, 16)], c_send.at[2])
        )

    wg_ref[:, 0:128] = c3_in[0:8, 0:16].astype(F32).reshape(128, 128)
    wg_ref[:, 128:256] = c3_in[8:16, 0:16].astype(F32).reshape(128, 128)
    bias_rows = c3_in[0, 16:32].astype(F32)
    bg_ref[:, 0:128] = bias_rows[0:1]
    bg_ref[:, 128:256] = bias_rows[1:2]

    for finish in pending:
        finish()


def hand_out(act_in, wg_in, bg_in, act_ref, wg_ref, bg_ref):
    act_ref[...] = act_in[...]
    wg_ref[...] = wg_in[...]
    bg_ref[...] = bg_in[...]


def shards(features, adj_tiles, tile_coords, tile_counts, weight, out_bias, out_grad):
    vmem = pl.BlockSpec(memory_space=pltpu.VMEM)
    dma = pltpu.SemaphoreType.DMA
    outs = (
        jax.ShapeDtypeStruct((128, 256), BF16),
        jax.ShapeDtypeStruct((128, 256), F32),
        jax.ShapeDtypeStruct((1, 256), F32),
    )
    results = pl.pallas_call(
        layer_kernel,
        name="layer",
        out_shape=outs,
        in_specs=[pl.BlockSpec(memory_space=pl.ANY)] * 7,
        out_specs=(vmem, vmem, vmem),
        scratch_shapes=[
            pltpu.VMEM((1, 4), jnp.int32),
            pltpu.VMEM((4, 2, 32), jnp.int32),
            pltpu.VMEM((128, 256), BF16),
            pltpu.VMEM((1, 256), F32),
            pltpu.VMEM((128, 256), BF16),
            pltpu.VMEM((129, 128, 128), BF16),
            pltpu.VMEM((4, 128), jnp.int32),
            pltpu.SMEM((4, 128), jnp.int32),
            pltpu.VMEM((8, 2, 128, 128), BF16),
            pltpu.VMEM((4, 2, 2, 2, 128, 128), BF16),
            pltpu.VMEM((8, 128, 128), F32),
            pltpu.VMEM((8, 128, 128), BF16),
            pltpu.VMEM((8, 128, 128), BF16),
            pltpu.VMEM((16, 16, 128), BF16),
            pltpu.VMEM((32, 16, 128), BF16),
            pltpu.VMEM((8, 128), F32),
            pltpu.VMEM((32, 8, 128), F32),
            pltpu.VMEM((8, 32, 128), BF16),
            pltpu.VMEM((16, 32, 128), BF16),
            dma((6,)),
            dma,
            dma((21,)),
            dma((8, 2)),
            dma((8, 2, 2)),
            dma((4,)),
            dma((4,)),
            dma((4,)),
            dma,
            dma,
            dma((5,)),
            dma((6,)),
        ],
        compiler_params=pltpu.CompilerParams(
            collective_id=1, has_side_effects=True, vmem_limit_bytes=60 << 20
        ),
        cost_estimate=pl.CostEstimate(
            flops=2 * 256 * 128**3, bytes_accessed=5 << 20, transcendentals=128 * 256
        ),
    )(
        tile_counts.reshape(1, 4),
        jnp.swapaxes(tile_coords[0, 0], 1, 2),
        features.reshape(8, 128, 128),
        adj_tiles.reshape(128, 128, 128),
        weight,
        out_bias.reshape(1, 256),
        out_grad,
    )
    activated, weight_grad, bias_grad = pl.pallas_call(
        hand_out,
        name="hand_out",
        out_shape=outs,
        in_specs=[vmem, vmem, vmem],
        out_specs=(vmem, vmem, vmem),
    )(*results)
    return activated, weight_grad, bias_grad.reshape(256)


def solution(mesh):
    placed = (
        P("row", None),
        P("row", "rep", None, None, None, None),
        P("row", "rep", None, None, None),
        P("row", "rep", None),
        P(),
        P(),
        P(("row", "rep"), None),
    )
    return jax.shard_map(
        shards,
        mesh=mesh,
        in_specs=placed,
        out_specs=(P(("row", "rep"), None), P(), P()),
        check_vma=False,
    )
```

time: 49.2 us -> 48.4 us (0.984)
  Pallas kernels: 48.4 us -> 47.6 us
    pallas_call x1, Pallas kernels: 46.8 us -> 46 us  [shards(): pl.pallas_call(layer_kernel, name='layer', out_shape=outs, in_specs=[pl.B...]
where the time goes in v4:
time: 48.4 us; the launch traced here: 48.2 us
  Pallas kernels  47.6 us (98%)
  between operations  0.64 us (1%)
    pallas_call x1, Pallas kernels, shards(): pl.pallas_call(layer_kernel, name='layer', out_shape=outs, in_specs=[pl.B...  46 us
    pallas_call x1, Pallas kernels, shards(): pl.pallas_call(hand_out, name='hand_out', out_shape=outs, in_specs=[vmem,...  1.59 us

profile of v4, /device:TPU:1, one launch (start us, length us, event | category | flops | bytes accessed | tf_op | source)
XLA Modules:
  0.0 48.2 jit_solution(13537230062324713295)
XLA Ops:
  0.6 46.0 %layer.1 = (bf16[128,256]{1,0:T(8,128)(2,1)}, f32[128,256]{1,0:T(8,128)}, f32[1,256]{1,0:T(1,128)}) custom-call(s32[1,4]{1,0:T(1,128)} %bitcast.12, s32[4,2,32]{2,1,0:T(2,128)} %bitcast.10, bf16[8,128,128]{2,1,0:T(8,128)(2,1)} %bitcast.9, bf16[128,128,128]{2,1,0:T(8,128)(2,1)} %bitcast.8, bf16[128,256]{1,0:T(8,128)(2,1)} %weight_hbm.1, f32[1,256]{1,0:T(1,128)} %bitcast.11, ...), custom_call_target="tpu_custom_call" | custom-call | flops 1073741824 | bytes 5242880 | tf_op jit(solution)/shard_map/layer/pallas_call | solution.py:478
  46.6 1.6 %hand_out.1 = (bf16[128,256]{1,0:T(8,128)(2,1)}, f32[128,256]{1,0:T(8,128)}, f32[1,256]{1,0:T(1,128)}) custom-call(bf16[128,256]{1,0:T(8,128)(2,1)} %get-tuple-element.9.act_in, f32[128,256]{1,0:T(8,128)} %get-tuple-element.10.wg_in, f32[1,256]{1,0:T(1,128)} %get-tuple-element.11.bg_in), custom_call_target="tpu_custom_call" | custom-call | tf_op jit(solution)/shard_map/hand_out/pallas_call | solution.py:532

commit v5 on v4

--- a/solution.py
+++ b/solution.py
@@ -163,13 +163,13 @@
         )
 
     def to_column(start):
-        parts = [(2, 1, 1), (6, 0, 1), (2, 0, 1), (6, 1, 1), (1, 0, 2), (7, 0, 2)]
+        parts = [(2, 1, 1), (6, 0, 1), (1, 0, 1), (7, 0, 1), (2, 0, 1), (6, 1, 1), (1, 1, 1), (7, 1, 1)]
         copies = [
             along_z(2 * n + to_core, dz, to_core, first, count)
             for n, (dz, first, count) in enumerate(parts)
             for to_core in (0, 1)
         ]
-        for copy in copies + [along_z(12, 0, 1 - core)]:
+        for copy in copies + [along_z(16, 0, 1 - core)]:
             copy.start() if start else copy.wait_send()
 
     pl.when(source)(lambda: (own_quarter().start(), to_column(True)) and None)
@@ -182,7 +182,7 @@
         side = 1 if dz == 6 else -1
         for n, far in enumerate((1, 2)):
             if far == 1 or half == (dz == 6):
-                send = a1_send.at[13 + (dz // 4) * 4 + half * 2 + n]
+                send = a1_send.at[17 + (dz // 4) * 4 + half * 2 + n]
                 copy = remote(piece, piece, send, a1_recv.at[src, half], device(0, 0, side * far, 0))
                 copy.start() if start else copy.wait_send()
 
@@ -216,7 +216,7 @@
         wait_bytes(held.at[src, pl.ds(first, count)], a1_recv.at[src, first])
 
     even_parts = [(0, 0, 2), (2, 0, 1), (6, 1, 1), (2, 1, 1), (6, 0, 1), (4, 0, 1), (4, 1, 1)]
-    odd_parts = [(1, 0, 2), (7, 0, 2), (3, 0, 1), (5, 1, 1), (3, 1, 1), (5, 0, 1)]
+    odd_parts = [(1, 0, 1), (7, 0, 1), (1, 1, 1), (7, 1, 1), (3, 0, 1), (5, 1, 1), (3, 1, 1), (5, 0, 1)]
 
     @pl.when(even)
     def _():
@@ -503,7 +503,7 @@
             pltpu.VMEM((16, 32, 128), BF16),
             dma((6,)),
             dma,
-            dma((21,)),
+            dma((25,)),
             dma((8, 2)),
             dma((8, 2, 2)),
             dma((4,)),

time: 48.4 us -> 47.6 us (0.983)
  Pallas kernels: 47.6 us -> 46.9 us
    pallas_call x1, Pallas kernels: 46 us -> 45.3 us  [shards(): pl.pallas_call(layer_kernel, name='layer', out_shape=outs, in_specs=[pl.B...]
where the time goes in v5:
time: 47.6 us; the launch traced here: 47.5 us
  Pallas kernels  46.9 us (99%)
  between operations  0.64 us (1%)
    pallas_call x1, Pallas kernels, shards(): pl.pallas_call(layer_kernel, name='layer', out_shape=outs, in_specs=[pl.B...  45.3 us
    pallas_call x1, Pallas kernels, shards(): pl.pallas_call(hand_out, name='hand_out', out_shape=outs, in_specs=[vmem,...  1.59 us

profile of v5, /device:TPU:1, one launch (start us, length us, event | category | flops | bytes accessed | tf_op | source)
XLA Modules:
  0.0 47.5 jit_solution(7031799638339560436)
XLA Ops:
  0.6 45.3 %layer.1 = (bf16[128,256]{1,0:T(8,128)(2,1)}, f32[128,256]{1,0:T(8,128)}, f32[1,256]{1,0:T(1,128)}) custom-call(s32[1,4]{1,0:T(1,128)} %bitcast.12, s32[4,2,32]{2,1,0:T(2,128)} %bitcast.10, bf16[8,128,128]{2,1,0:T(8,128)(2,1)} %bitcast.9, bf16[128,128,128]{2,1,0:T(8,128)(2,1)} %bitcast.8, bf16[128,256]{1,0:T(8,128)(2,1)} %weight_hbm.1, f32[1,256]{1,0:T(1,128)} %bitcast.11, ...), custom_call_target="tpu_custom_call" | custom-call | flops 1073741824 | bytes 5242880 | tf_op jit(solution)/shard_map/layer/pallas_call | solution.py:478
  45.9 1.6 %hand_out.1 = (bf16[128,256]{1,0:T(8,128)(2,1)}, f32[128,256]{1,0:T(8,128)}, f32[1,256]{1,0:T(1,128)}) custom-call(bf16[128,256]{1,0:T(8,128)(2,1)} %get-tuple-element.9.act_in, f32[128,256]{1,0:T(8,128)} %get-tuple-element.10.wg_in, f32[1,256]{1,0:T(1,128)} %get-tuple-element.11.bg_in), custom_call_target="tpu_custom_call" | custom-call | tf_op jit(solution)/shard_map/hand_out/pallas_call | solution.py:532

commit v6 on v5

--- a/solution.py
+++ b/solution.py
@@ -29,7 +29,6 @@
     cot_hbm,
     act_ref,
     wg_ref,
-    bg_ref,
     counts_ref,
     coords_ref,
     weight_ref,
@@ -299,17 +298,14 @@
         for r in tile_rows:
             total = acc[r] + products(r, sections, (core + turn) % 2)
             acc[r] = total
+            part_out[r] = total.astype(BF16)
         return carry
 
     pending.append(lambda: [pass_on(t, False) for t in range(4)])
-    lax.fori_loop(0, 3, add_products, 0)
-    for section in pair(3):
-        complete(section)
-    for r in tile_rows:
-        total = acc[r] + products(r, pair(3), 1 - core)
-        if r is not tile_rows[7]:
-            part_out[r] = total.astype(BF16)
-            remote(part_out.at[r], part_in.at[rep], b_send, b_recv, (row, r)).start()
+    lax.fori_loop(0, 4, add_products, 0)
+    for r in tile_rows[:7]:
+        remote(part_out.at[r], part_in.at[rep], b_send, b_recv, (row, r)).start()
+    total = acc[rep]
 
     for finish in pending:
         finish()
@@ -451,20 +447,19 @@
             lambda: wait_bytes(c3_in.at[pl.ds(0, 15), pl.ds(0, 16)], c_send.at[2])
         )
 
-    wg_ref[:, 0:128] = c3_in[0:8, 0:16].astype(F32).reshape(128, 128)
-    wg_ref[:, 128:256] = c3_in[8:16, 0:16].astype(F32).reshape(128, 128)
-    bias_rows = c3_in[0, 16:32].astype(F32)
+    wg_ref[...] = c3_in[...]
+
+    for finish in pending:
+        finish()
+
+
+def hand_out(act_in, pieces, act_ref, wg_ref, bg_ref):
+    act_ref[...] = act_in[...]
+    wg_ref[:, 0:128] = pieces[0:8, 0:16].astype(F32).reshape(128, 128)
+    wg_ref[:, 128:256] = pieces[8:16, 0:16].astype(F32).reshape(128, 128)
+    bias_rows = pieces[0, 16:32].astype(F32)
     bg_ref[:, 0:128] = bias_rows[0:1]
     bg_ref[:, 128:256] = bias_rows[1:2]
-
-    for finish in pending:
-        finish()
-
-
-def hand_out(act_in, wg_in, bg_in, act_ref, wg_ref, bg_ref):
-    act_ref[...] = act_in[...]
-    wg_ref[...] = wg_in[...]
-    bg_ref[...] = bg_in[...]
 
 
 def shards(features, adj_tiles, tile_coords, tile_counts, weight, out_bias, out_grad):
@@ -478,9 +473,9 @@
     results = pl.pallas_call(
         layer_kernel,
         name="layer",
-        out_shape=outs,
+        out_shape=(outs[0], jax.ShapeDtypeStruct((16, 32, 128), BF16)),
         in_specs=[pl.BlockSpec(memory_space=pl.ANY)] * 7,
-        out_specs=(vmem, vmem, vmem),
+        out_specs=(vmem, vmem),
         scratch_shapes=[
             pltpu.VMEM((1, 4), jnp.int32),
             pltpu.VMEM((4, 2, 32), jnp.int32),
@@ -533,7 +528,7 @@
         hand_out,
         name="hand_out",
         out_shape=outs,
-        in_specs=[vmem, vmem, vmem],
+        in_specs=[vmem, vmem],
         out_specs=(vmem, vmem, vmem),
     )(*results)
     return activated, weight_grad, bias_grad.reshape(256)

time: 47.6 us -> 47.5 us (level)
  no operation moved by 1% of the time
where the time goes in v6:
time: 47.5 us; the launch traced here: 47.3 us
  Pallas kernels  46.7 us (98%)
  between operations  0.64 us (1%)
    pallas_call x1, Pallas kernels, shards(): pl.pallas_call(layer_kernel, name='layer', out_shape=(outs[0], jax.ShapeD...  45.1 us
    pallas_call x1, Pallas kernels, shards(): pl.pallas_call(hand_out, name='hand_out', out_shape=outs, in_specs=[vmem,...  1.63 us

profile of v6, /device:TPU:1, one launch (start us, length us, event | category | flops | bytes accessed | tf_op | source)
XLA Modules:
  0.0 47.3 jit_solution(8305646775307460797)
XLA Ops:
  0.6 45.1 %layer.1 = (bf16[128,256]{1,0:T(8,128)(2,1)}, bf16[16,32,128]{2,1,0:T(8,128)(2,1)}) custom-call(s32[1,4]{1,0:T(1,128)} %bitcast.12, s32[4,2,32]{2,1,0:T(2,128)} %bitcast.10, bf16[8,128,128]{2,1,0:T(8,128)(2,1)} %bitcast.9, bf16[128,128,128]{2,1,0:T(8,128)(2,1)} %bitcast.8, bf16[128,256]{1,0:T(8,128)(2,1)} %weight_hbm.1, f32[1,256]{1,0:T(1,128)} %bitcast.11, ...), custom_call_target="tpu_custom_call" | custom-call | flops 1073741824 | bytes 5242880 | tf_op jit(solution)/shard_map/layer/pallas_call | solution.py:473
  45.7 1.6 %hand_out.1 = (bf16[128,256]{1,0:T(8,128)(2,1)}, f32[128,256]{1,0:T(8,128)}, f32[1,256]{1,0:T(1,128)}) custom-call(bf16[128,256]{1,0:T(8,128)(2,1)} %get-tuple-element.8.act_in, bf16[16,32,128]{2,1,0:T(8,128)(2,1)} %get-tuple-element.9.pieces), custom_call_target="tpu_custom_call" | custom-call | tf_op jit(solution)/shard_map/hand_out/pallas_call | solution.py:527

commit v7 on v6

--- a/solution.py
+++ b/solution.py
@@ -344,12 +344,12 @@
         place = c1_in.at[plane * 2 + core]
         return remote(c1_out.at[x2 * 4 + y2], place, c_send.at[0], c_recv.at[0], target)
 
-    @pl.when(jnp.logical_not(owner))
-    def _():
-        send_bias().start()
-
     for dx, dy in PLANE:
         send_piece(dx, dy).start()
+
+    @pl.when(jnp.logical_not(owner))
+    def _():
+        send_bias().start()
 
     @pl.when(active)
     def _():

time: 47.5 us -> 47.5 us (level)
  no operation moved by 1% of the time
where the time goes in v7:
time: 47.5 us; the launch traced here: 47.3 us
  Pallas kernels  46.7 us (98%)
  between operations  0.64 us (1%)
    pallas_call x1, Pallas kernels, shards(): pl.pallas_call(layer_kernel, name='layer', out_shape=(outs[0], jax.ShapeD...  45.1 us
    pallas_call x1, Pallas kernels, shards(): pl.pallas_call(hand_out, name='hand_out', out_shape=outs, in_specs=[vmem,...  1.63 us

profile of v7, /device:TPU:1, one launch (start us, length us, event | category | flops | bytes accessed | tf_op | source)
XLA Modules:
  0.0 47.3 jit_solution(10574182162947449682)
XLA Ops:
  0.6 45.1 %layer.1 = (bf16[128,256]{1,0:T(8,128)(2,1)}, bf16[16,32,128]{2,1,0:T(8,128)(2,1)}) custom-call(s32[1,4]{1,0:T(1,128)} %bitcast.12, s32[4,2,32]{2,1,0:T(2,128)} %bitcast.10, bf16[8,128,128]{2,1,0:T(8,128)(2,1)} %bitcast.9, bf16[128,128,128]{2,1,0:T(8,128)(2,1)} %bitcast.8, bf16[128,256]{1,0:T(8,128)(2,1)} %weight_hbm.1, f32[1,256]{1,0:T(1,128)} %bitcast.11, ...), custom_call_target="tpu_custom_call" | custom-call | flops 1073741824 | bytes 5242880 | tf_op jit(solution)/shard_map/layer/pallas_call | solution.py:473
  45.7 1.6 %hand_out.1 = (bf16[128,256]{1,0:T(8,128)(2,1)}, f32[128,256]{1,0:T(8,128)}, f32[1,256]{1,0:T(1,128)}) custom-call(bf16[128,256]{1,0:T(8,128)(2,1)} %get-tuple-element.8.act_in, bf16[16,32,128]{2,1,0:T(8,128)(2,1)} %get-tuple-element.9.pieces), custom_call_target="tpu_custom_call" | custom-call | tf_op jit(solution)/shard_map/hand_out/pallas_call | solution.py:527
